TPU v7x, 32 devices: a whole 2x2x4 slice. The times are simulated.
32 devices in a mesh: kv: 8 (over y, x, core), dp: 4 (over z).
Axes of the slice: x: 2, y: 2, z: 4, core: 2. Of those that a mesh axis runs over, the one named last changes fastest.
Arguments:
- queries: bfloat16 [32, 128, 576], P('dp'), may hold values from -48 to 48
- drafts: bfloat16 [32, 576], P('dp'), may hold values from -18 to 18
- cache: bfloat16 [8, 32768, 576], P('dp', 'kv'), may hold values from -4 to 4
- lengths: int32 [8], P('dp'), may hold values from 16384 to 32768, as said below
- row_seq: int32 [32], P('dp'), may hold values from 0 to 1, as said below
- row_pos: int32 [32], P('dp'), may hold values from 16384 to 32771, as said below
- w_uv: bfloat16 [128, 512, 128], P('kv'), may hold values from -0.25 to 0.25
- w_out: bfloat16 [16384, 7168], P('kv', 'dp'), may hold values from -0.046875 to 0.046875
- hidden: bfloat16 [32, 7168], P(None, 'dp'), may hold values from -0.59765625 to 0.59765625
- gain: float32 [7168], P('dp'), may hold values from 0.1 to 1.9
- w_gate: bfloat16 [7168, 18432], P('dp', 'kv'), may hold values from -0.0625 to 0.0625
- w_up: bfloat16 [7168, 18432], P('dp', 'kv'), may hold values from -0.0625 to 0.0625
- w_down: bfloat16 [18432, 7168], P('kv', 'dp'), may hold values from -0.01171875 to 0.01171875
Outputs:
- mixed: bfloat16 [32, 7168], P(None, 'dp')
Inputs may be any that keep to these rules, and one draw needn't show every extreme that they name: `lengths`: sequence 0 has exactly 32768 live positions. `row_seq`: each of a group's 2 sequences owns exactly 4 rows of the group, in any order. `row_pos`: A row's position is its sequence's length plus a step number; the 4 rows of one sequence take the step numbers 0 to 3 once each.
All inputs are finite; a program needn't handle non-finite values.
Results may differ from a plain program's by a relative error of at most 0.009.
Values may be sent and summed in bfloat16 or wider, within the bound.
No kernel may reach another device: no remote copies, remote signals or barrier semaphores. Data moves between devices by JAX's collectives and lax.ppermute only.
A program may use at most 128 MiB of HBM per device.

v0:
```python
import jax
import jax.numpy as jnp
from jax import lax
from jax.sharding import PartitionSpec as P

D = 7168
LAT = 512
ROPE = 64
HD = 128
SEQ_DP = 2
STEPS = 4


def scan_cache(query_rows, key_rows, live_len, block_len, block_count):
    qk_scale = (HD + ROPE) ** (-0.5)
    row_count = query_rows.shape[0]

    def visit(block_idx, carry):
        run_max, run_sum, weighted = carry
        key_block = lax.dynamic_slice_in_dim(key_rows, block_idx * block_len, block_len, 0)
        scores = (
            jnp.einsum("rc,kc->rk", query_rows, key_block, preferred_element_type=jnp.float32)
            * qk_scale
        )
        valid = block_idx * block_len + jnp.arange(block_len) < live_len
        scores = jnp.where(valid[None, :], scores, -1e30)
        new_max = jnp.maximum(run_max, jnp.max(scores, axis=1))
        weights = jnp.where(valid[None, :], jnp.exp(scores - new_max[:, None]), 0.0)
        factor = jnp.exp(run_max - new_max)
        run_sum = run_sum * factor + jnp.sum(weights, axis=1)
        weighted = weighted * factor[:, None] + jnp.dot(
            weights.astype(jnp.bfloat16), key_block[:, :LAT], preferred_element_type=jnp.float32
        )
        return (new_max, run_sum, weighted)

    start_carry = (
        jnp.full((row_count,), -1e30, jnp.float32),
        jnp.zeros((row_count,), jnp.float32),
        jnp.zeros((row_count, LAT), jnp.float32),
    )
    return lax.fori_loop(0, block_count, visit, start_carry)


def on_device(
    queries,
    drafts,
    cache,
    lengths,
    row_seq,
    row_pos,
    w_uv,
    w_out,
    hidden,
    gain,
    w_gate,
    w_up,
    w_down,
):
    kv_count = lax.axis_size("kv")
    kv_index = lax.axis_index("kv")
    tok_group, head_count = (queries.shape[0], queries.shape[1])
    head_local = head_count // kv_count
    ctx_dev = cache.shape[1]
    shard_start = kv_index * ctx_dev
    block_len = min(512, ctx_dev)
    block_total = ctx_dev // block_len
    qk_scale = (HD + ROPE) ** (-0.5)
    order_idx = jnp.arange(tok_group)
    same_seq = row_seq[:, None] == row_seq[None, :]
    rank_in_seq = jnp.sum(same_seq & (order_idx[:, None] > order_idx[None, :]), axis=1)
    picker = (row_seq[None, None, :] == jnp.arange(SEQ_DP)[:, None, None]) & (
        rank_in_seq[None, None, :] == jnp.arange(STEPS)[None, :, None]
    )
    picker_b = picker.astype(jnp.bfloat16)
    sorted_q = jnp.einsum(
        "sri,ihc->srhc", picker_b, queries, preferred_element_type=jnp.float32
    ).astype(jnp.bfloat16)
    sorted_drafts = (
        jnp.einsum("sri,ic->src", picker_b, drafts, preferred_element_type=jnp.float32)
        .astype(jnp.bfloat16)
        .reshape(tok_group, -1)
    )
    sorted_pos = jnp.sum(jnp.where(picker, row_pos[None, None, :], 0), axis=2).reshape(-1)
    sorted_seq = jnp.repeat(jnp.arange(SEQ_DP), STEPS)
    max_parts, sum_parts, acc_parts = ([], [], [])
    for seq_idx in range(SEQ_DP):
        live_len = lengths[seq_idx] - shard_start
        query_rows = sorted_q[seq_idx].reshape(STEPS * head_count, -1)
        run_max, run_sum, weighted = scan_cache(
            query_rows, cache[seq_idx], live_len, block_len, block_total
        )
        max_parts.append(run_max.reshape(STEPS, head_count))
        sum_parts.append(run_sum.reshape(STEPS, head_count))
        acc_parts.append(weighted.reshape(STEPS, head_count, LAT))
    local_max = jnp.concatenate(max_parts, axis=0)
    local_sum = jnp.concatenate(sum_parts, axis=0)
    local_acc = jnp.concatenate(acc_parts, axis=0)
    recv_acc, recv_max, recv_sum = (
        lax.all_to_all(local_acc[None], "kv", split_axis=2, concat_axis=0, tiled=True),
        lax.all_to_all(local_max[None], "kv", split_axis=2, concat_axis=0, tiled=True),
        lax.all_to_all(local_sum[None], "kv", split_axis=2, concat_axis=0, tiled=True),
    )
    head_max = jnp.max(recv_max, axis=0)
    rescale = jnp.exp(recv_max - head_max[None])
    head_acc = jnp.sum(recv_acc * rescale[..., None], axis=0)
    head_sum = jnp.sum(recv_sum * rescale, axis=0)
    head_q = lax.dynamic_slice_in_dim(
        sorted_q.reshape(tok_group, head_count, -1), kv_index * head_local, head_local, 1
    )
    draft_scores = (
        jnp.einsum("thc,jc->thj", head_q, sorted_drafts, preferred_element_type=jnp.float32)
        * qk_scale
    )
    draft_valid = (sorted_seq[:, None] == sorted_seq[None, :]) & (
        sorted_pos[None, :] <= sorted_pos[:, None]
    )
    draft_scores = jnp.where(draft_valid[:, None, :], draft_scores, -1e30)
    final_max = jnp.maximum(head_max, jnp.max(draft_scores, axis=2))
    adjust = jnp.exp(head_max - final_max)
    draft_weight = jnp.where(
        draft_valid[:, None, :], jnp.exp(draft_scores - final_max[:, :, None]), 0.0
    )
    denom = head_sum * adjust + jnp.sum(draft_weight, axis=2)
    numer = head_acc * adjust[:, :, None] + jnp.einsum(
        "thj,jl->thl",
        draft_weight.astype(jnp.bfloat16),
        sorted_drafts[:, :LAT],
        preferred_element_type=jnp.float32,
    )
    latent_sorted = (
        (numer / denom[:, :, None]).astype(jnp.bfloat16).reshape(SEQ_DP, STEPS, head_local, LAT)
    )
    latent_rows = jnp.einsum(
        "sri,srhl->ihl", picker_b, latent_sorted, preferred_element_type=jnp.float32
    ).astype(jnp.bfloat16)
    all_latents = lax.all_gather(latent_rows, "dp", axis=0, tiled=True)
    all_values = jnp.einsum(
        "thl,hlv->thv", all_latents, w_uv, preferred_element_type=jnp.float32
    ).astype(jnp.bfloat16)
    row_total = all_values.shape[0]
    attn_part = jnp.dot(
        all_values.reshape(row_total, head_local * HD), w_out, preferred_element_type=jnp.float32
    )
    attended = lax.psum(attn_part, "kv")
    resid = (hidden.astype(jnp.float32) + attended).astype(jnp.bfloat16)
    resid_f = resid.astype(jnp.float32)
    square_part = jnp.sum(resid_f * resid_f, axis=1)
    scaled = (resid_f * gain[None, :]).astype(jnp.bfloat16)
    gate_part = jnp.dot(scaled, w_gate, preferred_element_type=jnp.float32)
    up_part = jnp.dot(scaled, w_up, preferred_element_type=jnp.float32)
    gate_sum, up_sum, square_sum = lax.psum((gate_part, up_part, square_part), "dp")
    inv_rms = lax.rsqrt(square_sum / D + 1e-06)[:, None]
    act = (jax.nn.silu(gate_sum * inv_rms) * (up_sum * inv_rms)).astype(jnp.bfloat16)
    down_part = jnp.dot(act, w_down, preferred_element_type=jnp.float32)
    down_sum = lax.psum(down_part, "kv")
    return (resid_f + down_sum).astype(jnp.bfloat16)


def solution(mesh):
    placed = (
        P("dp", None, None),
        P("dp", None),
        P("dp", "kv", None),
        P("dp"),
        P("dp"),
        P("dp"),
        P("kv", None, None),
        P("kv", "dp"),
        P(None, "dp"),
        P("dp"),
        P("dp", "kv"),
        P("dp", "kv"),
        P("kv", "dp"),
    )
    return jax.shard_map(
        on_device, mesh=mesh, in_specs=placed, out_specs=P(None, "dp"), check_vma=False
    )
```

profile of v0, /device:TPU:0, one launch (start us, length us, event | category | flops | bytes accessed | tf_op | source)
XLA Modules:
  0.0 368.2 jit_solution(8215544242193573424)
XLA Ops:
  9.6 8.8 %fusion.69 = (bf16[1,4096,576]{1,2,0:T(8,128)(2,1)}, bf16[1,4096,576]{1,2,0:T(8,128)(2,1)}) fusion(bf16[2,4096,576]{1,2,0:T(8,128)(2,1)} %param.19), kind=kLoop, calls=%fused_computation.111 | loop fusion | bytes 18874368 | tf_op jit(solution)/shard_map/slice | solution.py:90
  18.4 7.7 %copy.124 = bf16[1,4096,576]{2,1,0:T(8,128)(2,1)} copy(bf16[1,4096,576]{1,2,0:T(8,128)(2,1)} %get-tuple-element.468) | data formatting | bytes 9437184
  31.4 40.9 %while.37 = (s32[]{:T(128)}, f32[512]{0:T(512)S(1)}, f32[512]{0:T(512)S(1)}, f32[512,512]{1,0:T(8,128)}, s32[]{:T(128)}, /*index=5*/bf16[4096,576]{1,0:T(8,128)(...) while((s32[]{:T(128)}, f32[512]{0:T(512)S(1)}, ...), condition=%wide.region_8.9_spmd.clone, body=%wide.region_5.0_spmd.clone.sunk | while | flops 573574656 | bytes 7112895 | solution.py:41
  38.4 3.0 convolution_add_fusion.6
  43.6 3.0 convolution_add_fusion.6
  48.7 3.0 convolution_add_fusion.6
  53.9 3.0 convolution_add_fusion.6
  59.0 3.0 convolution_add_fusion.6
  64.2 3.0 convolution_add_fusion.6
  73.0 7.7 %copy.123 = bf16[1,4096,576]{2,1,0:T(8,128)(2,1)} copy(bf16[1,4096,576]{1,2,0:T(8,128)(2,1)} %get-tuple-element.467) | data formatting | bytes 9437184
  82.2 40.8 %while.36 = (s32[]{:T(128)}, f32[512]{0:T(512)S(1)}, f32[512]{0:T(512)S(1)}, f32[512,512]{1,0:T(8,128)}, s32[]{:T(128)}, /*index=5*/bf16[4096,576]{1,0:T(8,128)(...) while((s32[]{:T(128)}, f32[512]{0:T(512)S(1)}, ...), condition=%wide.region_4.5_spmd.clone, body=%wide.region_1.4_spmd.clone.sunk | while | flops 573574656 | bytes 7112895 | solution.py:41
  125.1 5.2 %all-to-all-start.2 = ((f32[8,1,128]{2,1,0:T(1,128)}), f32[8,1,128]{2,1,0:T(1,128)S(1)}, u32[]{:S(2)}, u32[]{:S(2)}) async-start(f32[8,1,128]{2,1,0:T(1,128)} %reshape.201), calls=%async_computation.2 | async-start | bytes 8192 | tf_op jit(solution)/shard_map/all_to_all | solution.py:101
  134.9 3.3 all-to-all-start.1
  142.8 4.4 %all-to-all-start = ((f32[1,8,128,512]{3,1,0,2:T(8,128)}), f32[1,8,128,512]{3,1,0,2:T(8,128)}, u32[]{:S(2)}, u32[]{:S(2)}) async-start(f32[1,8,128,512]{3,1,0,2:T(8,128)} %copy.107), calls=%async_computation | async-start | bytes 4194304 | tf_op jit(solution)/shard_map/all_to_all | solution.py:99
  153.6 20.2 %all-to-all-done = f32[1,8,128,512]{3,1,0,2:T(8,128)} async-done(((f32[1,8,128,512]{3,1,0,2:T(8,128)}), f32[1,8,128,512]{3,1,0,2:T(8,128)}, u32[]{:S(2)}, u32[]{:S(2)}) %all-to-all-start) | async-done | bytes 2097184 | tf_op jit(solution)/shard_map/all_to_all | solution.py:99
  176.3 16.2 %all_gather.3 = bf16[32,16,512]{2,0,1:T(8,128)(2,1)S(1)} all-gather(bf16[8,16,512]{2,0,1:T(8,128)(2,1)S(1)} %fusion.30), channel_id=1, replica_groups=mesh['kv'=8,'dp'=4] {'dp'}, dimensions={0}, use_global_device_ids=true | all-gather | bytes 655360 | tf_op jit(solution)/shard_map/all_gather | solution.py:136
  192.9 5.2 %fusion.40 = f32[32,1792]{1,0:T(8,128)} fusion(bf16[2048,1792]{1,0:T(8,128)(2,1)} %param.24, bf16[16,4,8,128]{3,2,1,0:T(8,128)(2,1)S(1)} %fusion.31), kind=kOutput, calls=%fused_computation.68 | convolution fusion | flops 234881024 | bytes 7700480 | tf_op jit(solution)/shard_map/dot_general | solution.py:141
  198.3 51.6 %all-reduce.5.cloned.1.call-done = f32[32,1792]{1,0:T(8,128)} async-done(((f32[32,1792]{1,0:T(8,128)}), f32[32,1792]{1,0:T(8,128)}) %all-reduce.5.cloned.1.call-update) | async-done | bytes 229392 | tf_op jit(solution)/shard_map/psum | solution.py:144
  251.0 5.5 %fusion.44 = f32[32,2304]{1,0:T(8,128)} fusion(bf16[1792,2304]{1,0:T(8,128)(2,1)} %param.28, bf16[32,1792]{1,0:T(8,128)(2,1)S(1)} %get-tuple-element.458, f32[1792]{0:T(1024)S(1)} %copy-done.5), kind=kOutput, calls=%fused_computation.72 | convolution fusion | flops 264413184 | bytes 8674304 | tf_op jit(solution)/shard_map/dot_general | solution.py:150
  256.6 5.5 %fusion.46 = f32[32,2304]{1,0:T(8,128)} fusion(bf16[1792,2304]{1,0:T(8,128)(2,1)} %param.27, bf16[32,1792]{1,0:T(8,128)(2,1)S(1)} %get-tuple-element.458, f32[1792]{0:T(1024)S(1)} %copy-done.5), kind=kOutput, calls=%fused_computation.73 | convolution fusion | flops 264413184 | bytes 8674304 | tf_op jit(solution)/shard_map/dot_general | solution.py:149
  262.2 11.7 %psum.37 = f32[32]{0:T(128)S(1)} all-reduce(f32[32]{0:T(128)S(1)} %get-tuple-element.457), channel_id=1, replica_groups=mesh['kv'=8,'dp'=4] {'dp'}, use_global_device_ids=true, to_apply=%region_18.19 | all-reduce | flops 32 | bytes 256 | tf_op jit(solution)/shard_map/psum | solution.py:151
  273.9 28.8 %all-reduce.9.cloned.1.call-done = (f32[32,2304]{1,0:T(8,128)}, f32[32,2304]{1,0:T(8,128)}) async-done(((f32[32,2304]{1,0:T(8,128)}, f32[32,2304]{1,0:T(8,128)}), (f32[32,2304]{1,0:T(8,128)}, f32[32,2304]{1,0:T(8,128)})) %all-reduce.9.cloned.1.call-update) | async-done | bytes 589840 | tf_op jit(solution)/shard_map/psum | solution.py:151
  302.7 5.8 %fusion.37 = f32[32,1792]{1,0:T(8,128)} fusion(bf16[2304,1792]{1,0:T(8,128)(2,1)} %param.29, f32[32,2304]{1,0:T(8,128)} %get-tuple-element.451, f32[32,2304]{1,0:T(8,128)} %get-tuple-element.452, f32[32]{0:T(128)S(1)} %add_rsqrt_fusion), kind=kOutput, calls=%fused_computation.65 | convolution fusion | flops 264830976 | bytes 9076864 | tf_op jit(solution)/shard_map/dot_general | solution.py:154
  308.5 51.6 %all-reduce.7.cloned.1.call-done = f32[32,1792]{1,0:T(8,128)} async-done(((f32[32,1792]{1,0:T(8,128)}), f32[32,1792]{1,0:T(8,128)}) %all-reduce.7.cloned.1.call-update) | async-done | bytes 229392 | tf_op jit(solution)/shard_map/psum | solution.py:155
  (185 shorter events, 96.0 us)
Async XLA Ops:
  6.5 185.9 %copy-start = (bf16[16,512,128]{2,1,0:T(8,128)(2,1)S(1)}, bf16[16,512,128]{2,1,0:T(8,128)(2,1)}, u32[]{:S(2)}) copy-start(bf16[16,512,128]{2,1,0:T(8,128)(2,1)} %param.23) | copy-start | bytes 6291460
  18.4 7.8 %copy-start.4 = (bf16[8,128,576]{1,2,0:T(8,128)(2,1)S(1)}, bf16[8,128,576]{1,2,0:T(8,128)(2,1)}, u32[]{:S(2)}) copy-start(bf16[8,128,576]{1,2,0:T(8,128)(2,1)} %param.17) | copy-start | bytes 3538948
  27.1 1.0 copy-start.1
  73.0 7.7 %copy-start.3 = (bf16[1,4,128,576]{2,1,3,0:T(4,128)(2,1)S(1)}, bf16[1,4,128,576]{2,1,3,0:T(4,128)(2,1)}, u32[]{:S(2)}) copy-start(bf16[1,4,128,576]{2,1,3,0:T(4,128)(2,1)} %get-tuple-element.469) | copy-start | bytes 1769476
  125.1 9.8 %all-to-all-start.2 = ((f32[8,1,128]{2,1,0:T(1,128)}), f32[8,1,128]{2,1,0:T(1,128)S(1)}, u32[]{:S(2)}, u32[]{:S(2)}) async-start(f32[8,1,128]{2,1,0:T(1,128)} %reshape.201), calls=%async_computation.2 | async-start | bytes 8192 | tf_op jit(solution)/shard_map/all_to_all | solution.py:101
  134.9 7.9 %all-to-all-start.1 = ((f32[8,1,128]{2,1,0:T(1,128)}), f32[8,1,128]{2,1,0:T(1,128)S(1)}, u32[]{:S(2)}, u32[]{:S(2)}) async-start(f32[8,1,128]{2,1,0:T(1,128)} %reshape.199), calls=%async_computation.1 | async-start | bytes 8192 | tf_op jit(solution)/shard_map/all_to_all | solution.py:100
  139.9 7.3 %copy-start.2 = (bf16[2,4,128,576]{2,1,3,0:T(4,128)(2,1)S(1)}, bf16[2,4,128,576]{2,1,3,0:T(4,128)(2,1)}, u32[]{:S(2)}) copy-start(bf16[2,4,128,576]{2,1,3,0:T(4,128)(2,1)} %copy-done.1) | copy-start | bytes 3538948
  139.9 9.8 %copy-start.7 = (bf16[8,576]{1,0:T(8,128)(2,1)S(1)}, bf16[8,576]{1,0:T(8,128)(2,1)}, u32[]{:S(2)}) copy-start(bf16[8,576]{1,0:T(8,128)(2,1)} %param.18) | copy-start | bytes 27652
  139.9 10.0 %copy-start.8 = (s32[8]{0:T(128)S(1)}, s32[8]{0:T(128)}, u32[]{:S(2)}) copy-start(s32[8]{0:T(128)} %param.22) | copy-start | bytes 100
  142.8 31.0 %all-to-all-start = ((f32[1,8,128,512]{3,1,0,2:T(8,128)}), f32[1,8,128,512]{3,1,0,2:T(8,128)}, u32[]{:S(2)}, u32[]{:S(2)}) async-start(f32[1,8,128,512]{3,1,0,2:T(8,128)} %copy.107), calls=%async_computation | async-start | bytes 4194304 | tf_op jit(solution)/shard_map/all_to_all | solution.py:99
  147.2 102.8 %all-reduce.5.cloned.1.call-start = ((), (), s32[]{:S(2)}) async-start(), calls=%async_computation.3 | async-start | bytes 458752 | tf_op jit(solution)/shard_map/psum | solution.py:144
  192.5 57.5 %copy-start.6 = (bf16[32,1792]{1,0:T(8,128)(2,1)S(1)}, bf16[32,1792]{1,0:T(8,128)(2,1)}, u32[]{:S(2)}) copy-start(bf16[32,1792]{1,0:T(8,128)(2,1)} %param.25) | copy-start | bytes 344068
  192.9 58.1 %copy-start.5 = (f32[1792]{0:T(1024)S(1)}, f32[1792]{0:T(1024)}, u32[]{:S(2)}) copy-start(f32[1792]{0:T(1024)} %param.26) | copy-start | bytes 21508
  198.1 104.6 %all-reduce.9.cloned.1.call-start = ((), (), s32[]{:S(2)}) async-start(), calls=%async_computation.5 | async-start | bytes 1179648 | tf_op jit(solution)/shard_map/psum | solution.py:151
  262.1 98.0 %all-reduce.7.cloned.1.call-start = ((), (), s32[]{:S(2)}) async-start(), calls=%async_computation.4 | async-start | bytes 458752 | tf_op jit(solution)/shard_map/psum | solution.py:155
Sparse Core Ops, SparseCore 0:
  198.2 51.6 all-reduce.4
  262.2 40.4 all-reduce.8
  308.7 51.3 all-reduce.6
where the time goes:
time: 370 us; the launch traced here: 368 us
  waiting for transfers between devices  156 us (42%)
  matrix products  103 us (28%)
  local copies, waits for them, and re-layouts  38.7 us (10%)
  blocking collectives  27.9 us (8%)
  other arithmetic  15.1 us (4%)
  between operations  14.6 us (4%)
  starting transfers between devices  13.1 us (4%)
    psum x1, waiting for transfers between devices, on_device(): attended = lax.psum(attn_part, 'kv')  51.6 us
    psum x1, waiting for transfers between devices, on_device(): down_sum = lax.psum(down_part, 'kv')  51.6 us
    dot_general x16, matrix products, visit(): jnp.dot(weights.astype(jnp.bfloat16), key_block[:, :LAT], preferred_eleme...  46.8 us
    dot_general x16, matrix products, visit(): jnp.einsum('rc,kc->rk', query_rows, key_block, preferred_element_type=jnp...  30.6 us
    psum x1, waiting for transfers between devices, on_device(): lax.psum((gate_part, up_part, square_part), 'dp')  28.8 us
    unnamed x27, local copies, waits for them, and re-layouts  21.7 us
    all_to_all x1, waiting for transfers between devices, on_device(): lax.all_to_all(local_acc[None], 'kv', split_axis=2, concat_axis=0, tiled=...  20.2 us
    all_gather x1, blocking collectives, on_device(): all_latents = lax.all_gather(latent_rows, 'dp', axis=0, tiled=True)  16.2 us
  transfers between devices with their start and end apart: 6, of which 6 were waited for; matrix products, arithmetic and copies ran while one was open for 3% of the time, Pallas kernels for 0%

commit v1 on v0

--- a/solution.py
+++ b/solution.py
@@ -1,6 +1,10 @@
+import functools
+
 import jax
 import jax.numpy as jnp
 from jax import lax
+from jax.experimental import pallas as pl
+from jax.experimental.pallas import tpu as pltpu
 from jax.sharding import PartitionSpec as P
 
 D = 7168
@@ -156,6 +160,597 @@
     return (resid_f + down_sum).astype(jnp.bfloat16)
 
 
+CHUNK = 1024
+MASKED = -1e30
+F32 = jnp.float32
+BF16 = jnp.bfloat16
+SPEC_VMEM = pl.BlockSpec(memory_space=pltpu.VMEM)
+SPEC_SMEM = pl.BlockSpec(memory_space=pltpu.SMEM)
+SPEC_ANY = pl.BlockSpec(memory_space=pl.ANY)
+MIB = 1024 * 1024
+
+
+def dot_f32(lhs, rhs, contract=((1,), (0,))):
+    return lax.dot_general(lhs, rhs, (contract, ((), ())), preferred_element_type=F32)
+
+
+def held(array):
+    return pltpu.with_memory_space_constraint(array, pltpu.VMEM)
+
+
+def in_hbm(array):
+    return pltpu.with_memory_space_constraint(array, pltpu.HBM)
+
+
+def three_terms(exact):
+    high = exact.astype(BF16).astype(F32)
+    middle = (exact - high).astype(BF16).astype(F32)
+    low = (exact - high - middle).astype(BF16).astype(F32)
+    return high, middle, low
+
+
+def pack_logs(logs):
+    spread = jnp.concatenate(three_terms(logs) + (jnp.zeros_like(logs),), axis=1)
+    return jnp.concatenate([spread, jnp.zeros_like(spread)], axis=0).astype(BF16)
+
+
+def unpack_logs(spread, rows_in):
+    spread = spread.astype(F32)[:rows_in, :]
+    return spread[:, :128] + spread[:, 128:256] + spread[:, 256:384]
+
+
+def attention_kernel(
+    kv_count, weight_count, len_ref, seq_ref, pos_ref, draft_ref, query_hbm, key_hbm, *rest
+):
+    weights_hbm = rest[:weight_count]
+    mine_ref, theirs_ref = rest[weight_count : weight_count + 2]
+    weights_ref = rest[weight_count + 2 : 2 * weight_count + 2]
+    (query_t, keys, query_s, acc, row_max, row_sum, logs, query_sem, key_sem, weight_sem) = rest[
+        2 * weight_count + 2 :
+    ]
+    rows_in, width, head_count = query_hbm.shape
+    seqs, _, ctx = key_hbm.shape
+    steps = rows_in // seqs
+    head_local = head_count // kv_count
+    lat = acc.shape[1]
+    pair = 2 * CHUNK
+    pair_total = ctx // pair
+    factor = (HD + ROPE) ** (-0.5) * 1.4426950408889634
+    me = lax.axis_index("kv")
+    core = lax.rem(me, 2)
+
+    row_of = []
+    for s in range(seqs):
+        found = jnp.int32(0)
+        slots = [jnp.int32(0)] * steps
+        for r in range(rows_in):
+            mine = seq_ref[r] == s
+            slots = [jnp.where(mine & (found == i), r, slots[i]) for i in range(steps)]
+            found = found + mine.astype(jnp.int32)
+        row_of.append(slots)
+
+    def key_copy(s, c):
+        cols = pl.ds(pl.multiple_of(c * CHUNK, CHUNK), CHUNK)
+        return pltpu.make_async_copy(key_hbm.at[s, :, cols], keys.at[s, :, cols], key_sem.at[s, c])
+
+    def query_copy(s, i):
+        return pltpu.make_async_copy(
+            query_hbm.at[row_of[s][i]], query_t.at[s * steps + i], query_sem.at[s, i]
+        )
+
+    for i in range(steps):
+        query_copy(0, i).start()
+    later_copies = [key_copy(s, c) for s in range(seqs) for c in range(2 * pair_total)]
+    later_copies.pop(0).start()
+    later_copies += [query_copy(s, i) for s in range(1, seqs) for i in range(steps)]
+    weight_copies = [
+        pltpu.make_async_copy(weights_hbm[w], weights_ref[w], weight_sem.at[w]) for w in range(weight_count)
+    ]
+
+    def turn_queries(s, meanwhile=()):
+        for i in range(steps):
+            query_copy(s, i).wait()
+        for copy in meanwhile:
+            copy.start()
+        for i in range(steps):
+            query_s[s, i * head_count : (i + 1) * head_count, :] = query_t[s * steps + i].T
+
+    turn_queries(0, later_copies[:1])
+    for copy in later_copies[1:]:
+        copy.start()
+    weight_start = [(0, pair_total - 1) if w < 2 else (seqs - 1, 0) for w in range(weight_count)]
+
+    row_iota = lax.broadcasted_iota(jnp.int32, (rows_in, 128), 0)
+    owner = me == kv_count - 1
+    logs[...] = jnp.zeros_like(logs)
+
+    for s in range(seqs):
+        if s > 0:
+            turn_queries(s)
+
+        @pl.when(jnp.logical_not(owner))
+        def start_empty():
+            row_max[...] = jnp.full_like(row_max, MASKED)
+            row_sum[...] = jnp.zeros_like(row_sum)
+            acc[...] = jnp.zeros_like(acc)
+
+        @pl.when(owner)
+        def start_drafts():
+            draft_pad = jnp.concatenate(
+                [draft_ref[...].astype(F32), jnp.zeros((128 - rows_in, width), F32)], axis=0
+            ).astype(BF16)
+            lane = lax.broadcasted_iota(jnp.int32, (1, 128), 1)
+            score = dot_f32(query_s[s], draft_pad, ((1,), (1,)))
+            masks = []
+            for i in range(steps):
+                admitted = jnp.zeros((1, 128), jnp.int32)
+                for r in range(rows_in):
+                    fits = (seq_ref[r] == s) & (pos_ref[r] <= pos_ref[row_of[s][i]])
+                    admitted = jnp.where(lane == r, fits.astype(jnp.int32), admitted)
+                masks.append(jnp.broadcast_to(admitted, (head_count, 128)))
+            mask = jnp.concatenate(masks, axis=0) > 0
+            score = jnp.where(mask, score, MASKED)
+            first_max = jnp.broadcast_to(jnp.max(score, axis=1, keepdims=True), score.shape)
+            weight = jnp.where(mask, jnp.exp2((score - first_max) * factor), 0.0)
+            row_max[...] = first_max
+            row_sum[...] = weight
+            acc[...] = dot_f32(weight.astype(BF16), draft_pad[:, :lat])
+
+        live = jnp.clip(len_ref[s] - me * ctx, 0, ctx)
+        live_pairs = lax.div(live + (pair - 1), pair)
+
+        def add_pair_of_chunks(base, masked):
+            halves = [pl.ds(base, CHUNK), pl.ds(base + CHUNK, CHUNK)]
+            scores = []
+            for h in range(2):
+                key_copy(s, lax.div(base, CHUNK) + h).wait()
+                scores.append(dot_f32(query_s[s], keys[s, :, halves[h]]))
+            for h in range(2):
+                score = scores[h]
+                if masked:
+                    place = base + h * CHUNK + lax.broadcasted_iota(jnp.int32, (1, CHUNK), 1)
+                    score = jnp.where(place < live, score, MASKED)
+                old_max = row_max[...]
+                new_max = jnp.maximum(old_max, jnp.max(score, axis=1, keepdims=True))
+                scale = jnp.exp2((old_max - new_max) * factor)
+                weight = jnp.exp2((score - jnp.concatenate([new_max] * (CHUNK // 128), axis=1)) * factor)
+                part = weight[:, :128]
+                for c in range(1, CHUNK // 128):
+                    part = part + weight[:, c * 128 : (c + 1) * 128]
+                row_max[...] = new_max
+                row_sum[...] = row_sum[...] * scale + part
+                update = dot_f32(weight.astype(BF16), keys[s, :lat, halves[h]], ((1,), (1,)))
+                acc[...] = acc[...] * jnp.concatenate([scale] * (lat // 128), axis=1) + update
+
+        def visit(j, carry):
+            for copy, (at_seq, at_block) in zip(weight_copies, weight_start):
+                if at_seq == s:
+                    @pl.when(j == at_block)
+                    def start_weight(copy=copy):
+                        copy.start()
+            base = pl.multiple_of(j * pair, pair)
+            whole = base + pair <= live
+
+            @pl.when(whole)
+            def all_live():
+                add_pair_of_chunks(base, False)
+
+            @pl.when(jnp.logical_not(whole))
+            def some_live():
+                add_pair_of_chunks(base, True)
+
+            return carry
+
+        lax.fori_loop(0, live_pairs, visit, 0)
+
+        def skip(j, carry):
+            key_copy(s, 2 * j).wait()
+            key_copy(s, 2 * j + 1).wait()
+            return carry
+
+        lax.fori_loop(live_pairs, pair_total, skip, 0)
+        for copy, (at_seq, at_block) in zip(weight_copies, weight_start):
+            if at_seq == s:
+                @pl.when(live_pairs <= at_block)
+                def start_weight(copy=copy):
+                    copy.start()
+
+        total = jnp.sum(row_sum[...], axis=1, keepdims=True)
+        some = total > 0.0
+        acc[...] = acc[...] * jnp.where(some, 1.0 / jnp.where(some, total, 1.0), 0.0)
+        log_sum = jnp.where(
+            some, row_max[...] * factor + jnp.log2(jnp.where(some, total, 1.0)), MASKED
+        )
+        for i in range(steps):
+            flat = log_sum[i * head_count : (i + 1) * head_count, :].T[:1, :]
+            logs[...] = jnp.where(row_iota == row_of[s][i], flat, logs[...])
+            for b in range(kv_count // 2):
+                base = (b * rows_in + row_of[s][i]) * head_local
+                target = pl.ds(pl.multiple_of(base, head_local), head_local)
+                for ref, side in ((mine_ref, core), (theirs_ref, 1 - core)):
+                    start = i * head_count + (2 * b + side) * head_local
+                    source = pl.ds(pl.multiple_of(start, head_local), head_local)
+                    ref[target, :] = acc[source, :].astype(BF16)
+
+    spread = pack_logs(logs[...])
+    body = rows_in * head_count // 2
+    mine_ref[body:, :] = spread
+    theirs_ref[body:, :] = spread
+    for copy in weight_copies:
+        copy.wait()
+
+
+def attention(kv_count, lengths, row_seq, row_pos, drafts, query_t, key_t, weights):
+    rows_in, width, head_count = query_t.shape
+    seqs, _, ctx = key_t.shape
+    group = rows_in // seqs * head_count
+    message = pltpu.VMEM((rows_in * head_count // 2 + 16, LAT), BF16)
+    return pl.pallas_call(
+        functools.partial(attention_kernel, kv_count, len(weights)),
+        out_shape=[message] * 2 + [pltpu.VMEM(weight.shape, weight.dtype) for weight in weights],
+        in_specs=[SPEC_SMEM] * 3 + [SPEC_VMEM] + [SPEC_ANY] * (2 + len(weights)),
+        out_specs=[SPEC_VMEM] * 2 + [SPEC_ANY] * len(weights),
+        scratch_shapes=[
+            pltpu.VMEM(query_t.shape, BF16),
+            pltpu.VMEM(key_t.shape, BF16),
+            pltpu.VMEM((seqs, group, width), BF16),
+            pltpu.VMEM((group, LAT), F32),
+            pltpu.VMEM((group, 128), F32),
+            pltpu.VMEM((group, 128), F32),
+            pltpu.VMEM((rows_in, 128), F32),
+            pltpu.SemaphoreType.DMA((seqs, rows_in // seqs)),
+            pltpu.SemaphoreType.DMA((seqs, ctx // CHUNK)),
+            pltpu.SemaphoreType.DMA((len(weights),)),
+        ],
+        compiler_params=pltpu.CompilerParams(vmem_limit_bytes=26 * MIB),
+        cost_estimate=pl.CostEstimate(
+            flops=2 * seqs * group * ctx * (width + LAT),
+            bytes_accessed=2 * seqs * ctx * width,
+            transcendentals=seqs * group * ctx,
+        ),
+        name="attention",
+    )(*[in_hbm(arg) for arg in (lengths, row_seq, row_pos, drafts, query_t, key_t, *weights)])
+
+
+def merge_shares(logs):
+    peak = functools.reduce(jnp.maximum, logs)
+    shares = [jnp.exp2(log - peak) for log in logs]
+    total = functools.reduce(jnp.add, shares)
+    shares = [share / total for share in shares]
+    rows = sum(share.shape[0] for share in shares)
+    stacked = jnp.concatenate(shares + [jnp.zeros((128 - rows, 128), F32)], axis=0)
+    return stacked.T, peak + jnp.log2(total)
+
+
+def merge_pair_kernel(rows_in, heads, mine_ref, sibling_ref, *rest):
+    outs, mix = rest[:-1], rest[-1]
+    blocks = len(outs)
+    body = blocks * rows_in * heads
+    me = lax.axis_index("kv")
+    chip, core = lax.div(me, 2), lax.rem(me, 2)
+    parts = (mine_ref, sibling_ref)
+    mix[...], log_sum = merge_shares([unpack_logs(part[body:, :], rows_in) for part in parts])
+    spread = pack_logs(log_sum)
+    for k in range(blocks):
+        block = jnp.bitwise_xor(chip, k)
+        share = mix[pl.ds(pl.multiple_of((2 * block + core) * heads, heads), heads), :]
+        for r in range(rows_in):
+            source = pl.ds(pl.multiple_of((block * rows_in + r) * heads, heads), heads)
+            whole = jnp.zeros((heads, LAT), F32)
+            for p in range(2):
+                at = p * rows_in + r
+                whole = whole + parts[p][source, :].astype(F32) * share[:, at : at + 1]
+            outs[k][r * heads : (r + 1) * heads, :] = whole.astype(BF16)
+        outs[k][rows_in * heads :, :] = spread
+
+
+def merge_pair(rows_in, heads, mine, sibling):
+    blocks = (mine.shape[0] - 16) // (rows_in * heads)
+    message = jax.ShapeDtypeStruct((rows_in * heads + 16, LAT), BF16)
+    return pl.pallas_call(
+        functools.partial(merge_pair_kernel, rows_in, heads),
+        out_shape=[message] * blocks,
+        in_specs=[SPEC_VMEM] * 2,
+        out_specs=[SPEC_VMEM] * blocks,
+        scratch_shapes=[pltpu.VMEM((128, 128), F32)],
+        compiler_params=pltpu.CompilerParams(vmem_limit_bytes=8 * MIB),
+        name="merge_pair",
+    )(mine, sibling)
+
+
+def merge_values_kernel(rows_in, w_ref, *rest):
+    parts = rest[:-3]
+    out_ref, mix, latent = rest[-3:]
+    heads = w_ref.shape[0]
+    body = rows_in * heads
+    me = lax.axis_index("kv")
+    mix[...], _ = merge_shares([unpack_logs(part[body:, :], rows_in) for part in parts])
+    share = mix[pl.ds(pl.multiple_of(me * heads, heads), heads), :]
+    for r in range(rows_in):
+        block = slice(r * heads, (r + 1) * heads)
+        whole = jnp.zeros((heads, LAT), F32)
+        for k, part in enumerate(parts):
+            at = k * rows_in + r
+            whole = whole + part[block, :].astype(F32) * share[:, at : at + 1]
+        for c in range(LAT // 128):
+            latent[c, block, :] = whole[:, c * 128 : (c + 1) * 128]
+    for h in range(heads):
+        pieces = [latent[c, pl.ds(h, rows_in, stride=heads), :] for c in range(LAT // 128)]
+        rows = jnp.concatenate(pieces, axis=1).astype(BF16)
+        out_ref[:, h * HD : (h + 1) * HD] = dot_f32(rows, w_ref[h]).astype(BF16)
+
+
+def merge_values(rows_in, w_uv, parts):
+    heads = w_uv.shape[0]
+    return pl.pallas_call(
+        functools.partial(merge_values_kernel, rows_in),
+        out_shape=jax.ShapeDtypeStruct((rows_in, heads * HD), BF16),
+        in_specs=[SPEC_VMEM] * (1 + len(parts)),
+        out_specs=SPEC_VMEM,
+        scratch_shapes=[pltpu.VMEM((128, 128), F32), pltpu.VMEM((LAT // 128, rows_in * heads, 128), F32)],
+        compiler_params=pltpu.CompilerParams(vmem_limit_bytes=8 * MIB),
+        name="merge_values",
+    )(held(w_uv), *parts)
+
+
+def core_span(side, half):
+    core = lax.rem(lax.axis_index("kv"), 2)
+    return pl.ds(pl.multiple_of((core if side == 0 else 1 - core) * half, half), half)
+
+
+def project_theirs_kernel(flips, w_ref, *rest):
+    parts = rest[:-3]
+    rows_ref, theirs_ref, whole = rest[-3:]
+    rows = parts[0].shape[0]
+    at = lax.axis_index("dp")
+    for k, part in zip(flips, parts):
+        place = pl.ds(pl.multiple_of(jnp.bitwise_xor(at, k) * rows, rows), rows)
+        whole[place, :] = part[...].astype(F32)
+    stacked = whole[...].astype(BF16)
+    rows_ref[...] = stacked
+    theirs_ref[...] = dot_f32(stacked, w_ref[:, core_span(1, theirs_ref.shape[1])]).astype(BF16)
+
+
+def project_mine_kernel(w_ref, rows_ref, mine_ref):
+    mine_ref[...] = dot_f32(rows_ref[...], w_ref[:, core_span(0, mine_ref.shape[1])])
+
+
+def project(weight, parts, flips, name):
+    rows, depth = parts[0].shape
+    rows = rows * len(parts)
+    half = weight.shape[1] // 2
+    params = pltpu.CompilerParams(vmem_limit_bytes=8 * MIB)
+    cost = pl.CostEstimate(
+        flops=2 * rows * depth * half, bytes_accessed=2 * depth * half, transcendentals=0
+    )
+    stacked, theirs = pl.pallas_call(
+        functools.partial(project_theirs_kernel, flips),
+        out_shape=[jax.ShapeDtypeStruct((rows, depth), BF16), jax.ShapeDtypeStruct((rows, half), BF16)],
+        in_specs=[SPEC_VMEM] * (1 + len(parts)),
+        out_specs=[SPEC_VMEM] * 2,
+        scratch_shapes=[pltpu.VMEM((rows, depth), F32)],
+        compiler_params=params,
+        cost_estimate=cost,
+        name=name + "_theirs",
+    )(held(weight), *parts)
+    mine = pl.pallas_call(
+        project_mine_kernel,
+        out_shape=jax.ShapeDtypeStruct((rows, half), F32),
+        in_specs=[SPEC_VMEM] * 2,
+        out_specs=SPEC_VMEM,
+        compiler_params=params,
+        cost_estimate=cost,
+        name=name + "_mine",
+    )(held(weight), stacked)
+    return mine, theirs
+
+
+def add_pair_kernel(mine_ref, sibling_ref, out_ref):
+    out_ref[...] = (mine_ref[...] + sibling_ref[...].astype(F32)).astype(BF16)
+
+
+def add_pair(mine, sibling):
+    return pl.pallas_call(
+        add_pair_kernel,
+        out_shape=jax.ShapeDtypeStruct(mine.shape, BF16),
+        in_specs=[SPEC_VMEM] * 2,
+        out_specs=SPEC_VMEM,
+        compiler_params=pltpu.CompilerParams(vmem_limit_bytes=4 * MIB),
+        name="add_pair",
+    )(mine, sibling)
+
+
+def add_tree(parts):
+    parts = [part[...].astype(F32) for part in parts]
+    while len(parts) > 1:
+        parts = [parts[i] + parts[i + 1] for i in range(0, len(parts), 2)]
+    return parts[0]
+
+
+def add_chips_kernel(base_ref, *rest):
+    parts, out_ref = rest[:-1], rest[-1]
+    half = out_ref.shape[1]
+    base = base_ref[...]
+    if base.shape[1] > half:
+        core = lax.rem(lax.axis_index("kv"), 2)
+        base = jnp.where(core == 0, base[:, :half].astype(F32), base[:, half:].astype(F32))
+    out_ref[...] = (base.astype(F32) + add_tree(parts)).astype(BF16)
+
+
+def add_chips(base, parts, name):
+    return pl.pallas_call(
+        add_chips_kernel,
+        out_shape=jax.ShapeDtypeStruct(parts[0].shape, BF16),
+        in_specs=[SPEC_VMEM] * (1 + len(parts)),
+        out_specs=SPEC_VMEM,
+        compiler_params=pltpu.CompilerParams(vmem_limit_bytes=4 * MIB),
+        name=name,
+    )(base, *parts)
+
+
+def expand_half(side, gate_ref, up_ref, gain_ref, resid):
+    half = resid.shape[1]
+    span = core_span(side, half)
+    scaled = (resid * gain_ref[:, span]).astype(BF16)
+    square = jnp.sum(resid * resid, axis=1, keepdims=True)
+    return dot_f32(scaled, gate_ref[span, :]), dot_f32(scaled, up_ref[span, :]), square
+
+
+def expand_mine_kernel(gate_ref, up_ref, gain_ref, mine_ref, sums_ref, square_ref):
+    width = gate_ref.shape[1]
+    gate, up, square = expand_half(0, gate_ref, up_ref, gain_ref, mine_ref[...].astype(F32))
+    sums_ref[:, :width] = gate
+    sums_ref[:, width:] = up
+    square_ref[...] = jnp.broadcast_to(square, square_ref.shape)
+
+
+def expand_rest_kernel(gate_ref, up_ref, gain_ref, sibling_ref, sums_ref, square_ref, *rest):
+    outs, total = rest[:-1], rest[-1]
+    rows = outs[0].shape[0]
+    width = gate_ref.shape[1]
+    at = lax.axis_index("dp")
+    gate, up, square = expand_half(1, gate_ref, up_ref, gain_ref, sibling_ref[...].astype(F32))
+    total[:, :width] = sums_ref[:, :width] + gate
+    total[:, width : 2 * width] = sums_ref[:, width:] + up
+    lane = lax.broadcasted_iota(jnp.int32, square_ref.shape, 1)
+    terms = three_terms(square_ref[...] + square)
+    tail = jnp.zeros(lane.shape, F32)
+    for t in range(3):
+        tail = jnp.where(lane == t, terms[t], tail)
+    total[:, 2 * width :] = tail
+    for k in range(len(outs)):
+        place = pl.ds(pl.multiple_of(jnp.bitwise_xor(at, k) * rows, rows), rows)
+        outs[k][...] = total[place, :].astype(BF16)
+
+
+def expand(dp_count, w_gate, w_up, gain, mine, sibling):
+    cols, width = w_gate.shape
+    rows = mine.shape[0]
+    params = pltpu.CompilerParams(vmem_limit_bytes=8 * MIB)
+    cost = pl.CostEstimate(
+        flops=2 * rows * cols * width, bytes_accessed=2 * cols * width, transcendentals=0
+    )
+    weights = (held(w_gate), held(w_up), gain.reshape(1, cols))
+    sums, square = pl.pallas_call(
+        expand_mine_kernel,
+        out_shape=[
+            jax.ShapeDtypeStruct((rows, 2 * width), F32),
+            jax.ShapeDtypeStruct((rows, 128), F32),
+        ],
+        in_specs=[SPEC_VMEM] * 4,
+        out_specs=[SPEC_VMEM] * 2,
+        compiler_params=params,
+        cost_estimate=cost,
+        name="gate_up_mine",
+    )(*weights, mine)
+    message = jax.ShapeDtypeStruct((rows // dp_count, 2 * width + 128), BF16)
+    return pl.pallas_call(
+        expand_rest_kernel,
+        out_shape=[message] * dp_count,
+        in_specs=[SPEC_VMEM] * 6,
+        out_specs=[SPEC_VMEM] * dp_count,
+        scratch_shapes=[pltpu.VMEM((rows, 2 * width + 128), F32)],
+        compiler_params=params,
+        cost_estimate=cost,
+        name="gate_up_rest",
+    )(*weights, sibling, sums, square)
+
+
+def activate_kernel(*rest):
+    parts, out_ref = rest[:-1], rest[-1]
+    width = out_ref.shape[1]
+    total = functools.reduce(jnp.add, [part[...].astype(F32) for part in parts])
+    square = jnp.sum(total[:, 2 * width :], axis=1, keepdims=True)
+    inv_rms = lax.rsqrt(square / D + 1e-06)
+    gate = total[:, :width] * inv_rms
+    up = total[:, width : 2 * width] * inv_rms
+    out_ref[...] = (gate / (1.0 + jnp.exp(-gate)) * up).astype(BF16)
+
+
+def activate(parts):
+    rows, wide = parts[0].shape
+    return pl.pallas_call(
+        activate_kernel,
+        out_shape=jax.ShapeDtypeStruct((rows, (wide - 128) // 2), BF16),
+        in_specs=[SPEC_VMEM] * len(parts),
+        out_specs=SPEC_VMEM,
+        compiler_params=pltpu.CompilerParams(vmem_limit_bytes=4 * MIB),
+        name="activate",
+    )(*parts)
+
+
+def assemble_kernel(mine_ref, sibling_ref, out_ref):
+    half = mine_ref.shape[1]
+    left = lax.rem(lax.axis_index("kv"), 2) == 0
+    mine, sibling = mine_ref[...].astype(F32), sibling_ref[...].astype(F32)
+    out_ref[:, :half] = jnp.where(left, mine, sibling).astype(BF16)
+    out_ref[:, half:] = jnp.where(left, sibling, mine).astype(BF16)
+
+
+def assemble(mine, sibling):
+    rows, half = mine.shape
+    return pl.pallas_call(
+        assemble_kernel,
+        out_shape=jax.ShapeDtypeStruct((rows, 2 * half), BF16),
+        in_specs=[SPEC_VMEM] * 2,
+        out_specs=SPEC_VMEM,
+        compiler_params=pltpu.CompilerParams(vmem_limit_bytes=4 * MIB),
+        name="assemble",
+    )(mine, sibling)
+
+
+def partner(array, axis, flip):
+    pairs = [(i, i ^ flip) for i in range(lax.axis_size(axis))]
+    return lax.ppermute(array, axis, pairs)
+
+
+def swap(parts, axis, unit, flips):
+    return [partner(parts[k], axis, k * unit) if k else parts[0] for k in flips]
+
+
+def line_flips(count):
+    return [*range(2, count), 1, 0]
+
+
+def grid_flips(count):
+    return list(range(count - 1, -1, -1))
+
+
+def sum_over_kv(weight, parts, flips, base, name):
+    chips = lax.axis_size("kv") // 2
+    mine, theirs = project(weight, parts, flips, name)
+    pair = add_pair(mine, partner(theirs, "kv", 1))
+    half = add_chips(base, swap([pair] * chips, "kv", 2, range(chips)), name + "_sum")
+    return half, partner(half, "kv", 1)
+
+
+def on_device_tiled(
+    queries, drafts, cache, lengths, row_seq, row_pos, w_uv, w_out, hidden, gain, w_gate, w_up, w_down
+):
+    kv_count = lax.axis_size("kv")
+    dp_count = lax.axis_size("dp")
+    rows_in, head_count = queries.shape[:2]
+    flips = line_flips(dp_count)
+    query_t = jnp.swapaxes(queries, 1, 2)
+    key_t = jnp.swapaxes(cache, 1, 2)
+    mine, theirs, w_uv, w_out, w_gate, w_up = attention(
+        kv_count, lengths, row_seq, row_pos, drafts, query_t, key_t, [w_uv, w_out, w_gate, w_up]
+    )
+    blocks = merge_pair(rows_in, head_count // kv_count, mine, partner(theirs, "kv", 1))
+    values = merge_values(rows_in, w_uv, swap(blocks, "kv", 2, grid_flips(len(blocks))))
+    resid, resid_sibling = sum_over_kv(w_out, swap([values] * dp_count, "dp", 1, flips), flips, hidden, "project_out")
+    sums = expand(dp_count, w_gate, w_up, gain, resid, resid_sibling)
+    act = activate(swap(sums, "dp", 1, flips))
+    mixed, mixed_sibling = sum_over_kv(w_down, swap([act] * dp_count, "dp", 1, flips), flips, resid, "project_down")
+    return assemble(mixed, mixed_sibling)
+
+
+def tiles_fit(kv_count, dp_count, head_count, rows_in, cols, ctx):
+    powers = kv_count & (kv_count - 1) == 0 and dp_count & (dp_count - 1) == 0
+    heads = head_count % (16 * kv_count) == 0 and head_count == 128 and kv_count * rows_in <= 128
+    return powers and heads and rows_in == 8 and cols % 256 == 0 and ctx % (2 * CHUNK) == 0
+
+
 def solution(mesh):
     placed = (
         P("dp", None, None),
@@ -172,6 +767,23 @@
         P("dp", "kv"),
         P("kv", "dp"),
     )
-    return jax.shard_map(
-        on_device, mesh=mesh, in_specs=placed, out_specs=P(None, "dp"), check_vma=False
-    )
+
+    def placed_call(body):
+        return jax.shard_map(
+            body, mesh=mesh, in_specs=placed, out_specs=P(None, "dp"), check_vma=False
+        )
+
+    def run(*args):
+        kv_count, dp_count = mesh.shape["kv"], mesh.shape["dp"]
+        queries, cache, hidden = args[0], args[2], args[8]
+        fits = tiles_fit(
+            kv_count,
+            dp_count,
+            queries.shape[1],
+            queries.shape[0] // dp_count,
+            hidden.shape[1] // dp_count,
+            cache.shape[1] // kv_count,
+        )
+        return placed_call(on_device_tiled if fits else on_device)(*args)
+
+    return run

time: 370 us -> 81.5 us (0.22)
  waiting for transfers between devices: 156 us -> 32.2 us
  matrix products: 103 us -> 0 us
  local copies, waits for them, and re-layouts: 38.7 us -> 0.03 us
  blocking collectives: 27.9 us -> 0 us
  Pallas kernels: 0 us -> 24.9 us
  other arithmetic: 15.1 us -> 0.01 us
  between operations: 14.6 us -> 0.17 us
  starting transfers between devices: 13.1 us -> 24 us
    psum x3 -> x0, waiting for transfers between devices: 132 us -> none  [the longest x1 51.6 us: on_device(): attended = lax.psum(attn_part, 'kv')]
    dot_general x42 -> x0, matrix products: 103 us -> none  [the longest x16 46.8 us: visit(): jnp.dot(weights.astype(jnp.bfloat16), key_block[:, :LAT], preferred_eleme...]
    ppermute x0 -> x23, waiting for transfers between devices: none -> 32.2 us  [partner(): return lax.ppermute(array, axis, pairs)]
    pallas_call x0 -> x15, Pallas kernels: none -> 24.9 us  [the longest x1 16.8 us: attention(): pl.pallas_call(functools.partial(attention_kernel, kv_count, len(weights)...]
    ppermute x0 -> x23, starting transfers between devices: none -> 24 us  [partner(): return lax.ppermute(array, axis, pairs)]
    all_to_all x3 -> x0, waiting for transfers between devices: 23.5 us -> none  [the longest x1 20.2 us: on_device(): lax.all_to_all(local_acc[None], 'kv', split_axis=2, concat_axis=0, tiled=...]
    unnamed x27 -> x8, local copies, waits for them, and re-layouts: 21.7 us -> 0.03 us
    all_gather x1 -> x0, blocking collectives: 16.2 us -> none  [on_device(): all_latents = lax.all_gather(latent_rows, 'dp', axis=0, tiled=True)]
  transfers between devices with their start and end apart: 6 -> 23, of which waited for: 6 -> 20; matrix products, arithmetic and copies ran while one was open for 3% -> 0% of each run, Pallas kernels for 0% -> 4%
where the time goes in v1:
time: 81.5 us; the launch traced here: 81.4 us
  waiting for transfers between devices  32.2 us (40%)
  Pallas kernels  24.9 us (31%)
  starting transfers between devices  24 us (29%)
    ppermute x23, waiting for transfers between devices, partner(): return lax.ppermute(array, axis, pairs)  32.2 us
    ppermute x23, starting transfers between devices, partner(): return lax.ppermute(array, axis, pairs)  24 us
    pallas_call x1, Pallas kernels, attention(): pl.pallas_call(functools.partial(attention_kernel, kv_count, len(weights)...  16.8 us
  transfers between devices with their start and end apart: 23, of which 20 were waited for; matrix products, arithmetic and copies ran while one was open for 0% of the time, Pallas kernels for 4%

profile of v1, /device:TPU:0, one launch (start us, length us, event | category | flops | bytes accessed | tf_op | source)
XLA Modules:
  0.0 81.4 jit_solution(7214251545436561597)
XLA Ops:
  0.0 16.8 %attention.1 = (bf16[528,512]{1,0:T(8,128)(2,1)S(1)}, bf16[528,512]{1,0:T(8,128)(2,1)S(1)}, bf16[16,512,128]{2,1,0:T(8,128)(2,1)S(1)}, bf16[2048,1792]{1,0:T(8,1...) custom-call(s32[2]{0:T(128)} %len_ref.1, s32[8]{0:T(128)} %seq_ref.1, s32[8]{0:T(128)} %pos_ref.1, ...), custom_call_target="tpu_custom_call" | custom-call | flops 9126805504 | bytes 9437184 | tf_op jit(solution)/shard_map/attention/pallas_call | solution.py:388
  17.3 1.6 %collective-permute-done.sibling_ref = bf16[528,512]{1,0:T(8,128)(2,1)S(1)} collective-permute-done((bf16[528,512]{1,0:T(8,128)(2,1)S(1)}, bf16[528,512]{1,0:T(8,128)(2,1)S(1)}, u32[]{:S(2)}, u32[]{:S(2)}) %collective-permute-start) | collective-permute-done | bytes 540704 | tf_op jit(solution)/shard_map/ppermute | solution.py:704
  19.3 3.9 %collective-permute-start.1 = (bf16[144,512]{1,0:T(8,128)(2,1)S(1)}, bf16[144,512]{1,0:T(8,128)(2,1)S(1)}, u32[]{:S(2)}, u32[]{:S(2)}) collective-permute-start(bf16[144,512]{1,0:T(8,128)(2,1)S(1)} %get-tuple-element.29), channel_id=1, source_target_pairs={{0,24},{4,28},{8,16},{12,20},{16,8},{20,12},{24,0},{28,4},{1,25},{... | collective-permute-start | bytes 442376 | tf_op jit(solution)/shard_map/ppermute | solution.py:704
  23.9 4.0 %collective-permute-done.1.rest_0_ = bf16[144,512]{1,0:T(8,128)(2,1)S(1)} collective-permute-done((bf16[144,512]{1,0:T(8,128)(2,1)S(1)}, bf16[144,512]{1,0:T(8,128)(2,1)S(1)}, u32[]{:S(2)}, u32[]{:S(2)}) %collective-permute-start.1) | collective-permute-done | bytes 147488 | tf_op jit(solution)/shard_map/ppermute | solution.py:704
  27.9 2.9 %collective-permute-done.2.rest_1_ = bf16[144,512]{1,0:T(8,128)(2,1)S(1)} collective-permute-done((bf16[144,512]{1,0:T(8,128)(2,1)S(1)}, bf16[144,512]{1,0:T(8,128)(2,1)S(1)}, u32[]{:S(2)}, u32[]{:S(2)}) %collective-permute-start.2) | collective-permute-done | bytes 147488 | tf_op jit(solution)/shard_map/ppermute | solution.py:704
  31.5 2.6 %collective-permute-start.4 = (bf16[8,2048]{1,0:T(8,128)(2,1)S(1)}, bf16[8,2048]{1,0:T(8,128)(2,1)S(1)}, u32[]{:S(2)}, u32[]{:S(2)}) collective-permute-start(bf16[8,2048]{1,0:T(8,128)(2,1)S(1)} %merge_values.1.rest_3_), channel_id=1, source_target_pairs={{0,2},{1,3},{2,0},{3,1},{4,6},{5,7},{6,4},{7,5},{8,10},{9,11},{10,... | collective-permute-start | bytes 98312 | tf_op jit(solution)/shard_map/ppermute | solution.py:704
  34.0 1.6 %collective-permute-start.5 = (bf16[8,2048]{1,0:T(8,128)(2,1)S(1)}, bf16[8,2048]{1,0:T(8,128)(2,1)S(1)}, u32[]{:S(2)}, u32[]{:S(2)}) collective-permute-start(bf16[8,2048]{1,0:T(8,128)(2,1)S(1)} %merge_values.1.rest_3_), channel_id=1, source_target_pairs={{0,3},{1,2},{2,1},{3,0},{4,7},{5,6},{6,5},{7,4},{8,11},{9,10},{10,... | collective-permute-start | bytes 98312 | tf_op jit(solution)/shard_map/ppermute | solution.py:704
  36.7 3.1 %collective-permute-done.5.rest_1_ = bf16[8,2048]{1,0:T(8,128)(2,1)S(1)} collective-permute-done((bf16[8,2048]{1,0:T(8,128)(2,1)S(1)}, bf16[8,2048]{1,0:T(8,128)(2,1)S(1)}, u32[]{:S(2)}, u32[]{:S(2)}) %collective-permute-start.5) | collective-permute-done | bytes 32800 | tf_op jit(solution)/shard_map/ppermute | solution.py:704
  42.0 1.6 %collective-permute-start.10 = (bf16[32,896]{1,0:T(8,128)(2,1)S(1)}, bf16[32,896]{1,0:T(8,128)(2,1)S(1)}, u32[]{:S(2)}, u32[]{:S(2)}) collective-permute-start(bf16[32,896]{1,0:T(8,128)(2,1)S(1)} %add_pair.2.rest_0_), channel_id=1, source_target_pairs={{0,24},{4,28},{8,16},{12,20},{16,8},{20,12},{24,0},{28,4},{1,25},{... | collective-permute-start | bytes 172040 | tf_op jit(solution)/shard_map/ppermute | solution.py:704
  45.5 2.2 %collective-permute-done.10.rest_3_ = bf16[32,896]{1,0:T(8,128)(2,1)S(1)} collective-permute-done((bf16[32,896]{1,0:T(8,128)(2,1)S(1)}, bf16[32,896]{1,0:T(8,128)(2,1)S(1)}, u32[]{:S(2)}, u32[]{:S(2)}) %collective-permute-start.10) | collective-permute-done | bytes 57376 | tf_op jit(solution)/shard_map/ppermute | solution.py:704
  48.9 1.5 %gate_up_mine.1 = (f32[32,4608]{1,0:T(8,128)S(1)}, f32[32,128]{1,0:T(8,128)S(1)}) custom-call(bf16[1792,2304]{1,0:T(8,128)(2,1)S(1)} %get-tuple-element.35.gate_ref, bf16[1792,2304]{1,0:T(8,128)(2,1)S(1)} %get-tuple-element.36.up_ref, f32[1,1792]{1,0:T(1,128)S(1)} %reshape.3.gain_ref, bf16[32,896]{1,0:T(8,128)(2,1)S(1)} %project_out_sum.1.mine_ref.base_ref), custom_call_target="tpu_custom_call" | custom-call | flops 264241152 | bytes 8257536 | tf_op jit(solution)/shard_map/gate_up_mine/pallas_call | solution.py:634
  50.5 1.6 %gate_up_rest.1 = (bf16[8,4736]{1,0:T(8,128)(2,1)S(1)}, bf16[8,4736]{1,0:T(8,128)(2,1)S(1)}, bf16[8,4736]{1,0:T(8,128)(2,1)S(1)}, bf16[8,4736]{1,0:T(8,128)(2,1)S(1)}) custom-call(bf16[1792,2304]{1,0:T(8,128)(2,1)S(1)} %get-tuple-element.35.gate_ref, bf16[1792,2304]{1,0:T(8,128)(2,1)S(1)} %get-tuple-element.36.up_ref, f32[1,1792]{1,0:T(1,128)S(1)} %reshape.3.gain_ref, ...), custom_call_target="tpu_custom_call" | custom-call | flops 264241152 | bytes 8257536 | tf_op jit(solution)/shard_map/gate_up_rest/pallas_call | solution.py:647
  52.1 1.8 %collective-permute-start.12 = (bf16[8,4736]{1,0:T(8,128)(2,1)S(1)}, bf16[8,4736]{1,0:T(8,128)(2,1)S(1)}, u32[]{:S(2)}, u32[]{:S(2)}) collective-permute-start(bf16[8,4736]{1,0:T(8,128)(2,1)S(1)} %get-tuple-element.39), channel_id=1, source_target_pairs={{0,2},{1,3},{2,0},{3,1},{4,6},{5,7},{6,4},{7,5},{8,10},{9,11},{10,... | collective-permute-start | bytes 227336 | tf_op jit(solution)/shard_map/ppermute | solution.py:704
  53.8 1.0 %collective-permute-start.13 = (bf16[8,4736]{1,0:T(8,128)(2,1)S(1)}, bf16[8,4736]{1,0:T(8,128)(2,1)S(1)}, u32[]{:S(2)}, u32[]{:S(2)}) collective-permute-start(bf16[8,4736]{1,0:T(8,128)(2,1)S(1)} %get-tuple-element.40), channel_id=1, source_target_pairs={{0,3},{1,2},{2,1},{3,0},{4,7},{5,6},{6,5},{7,4},{8,11},{9,10},{10,... | collective-permute-start | bytes 227336 | tf_op jit(solution)/shard_map/ppermute | solution.py:704
  55.6 5.3 %collective-permute-done.12.rest_0_ = bf16[8,4736]{1,0:T(8,128)(2,1)S(1)} collective-permute-done((bf16[8,4736]{1,0:T(8,128)(2,1)S(1)}, bf16[8,4736]{1,0:T(8,128)(2,1)S(1)}, u32[]{:S(2)}, u32[]{:S(2)}) %collective-permute-start.12) | collective-permute-done | bytes 75808 | tf_op jit(solution)/shard_map/ppermute | solution.py:704
  60.9 1.3 %collective-permute-done.14.rest_2_ = bf16[8,4736]{1,0:T(8,128)(2,1)S(1)} collective-permute-done((bf16[8,4736]{1,0:T(8,128)(2,1)S(1)}, bf16[8,4736]{1,0:T(8,128)(2,1)S(1)}, u32[]{:S(2)}, u32[]{:S(2)}) %collective-permute-start.14) | collective-permute-done | bytes 75808 | tf_op jit(solution)/shard_map/ppermute | solution.py:704
  62.3 1.5 %collective-permute-start.15 = (bf16[8,2304]{1,0:T(8,128)(2,1)S(1)}, bf16[8,2304]{1,0:T(8,128)(2,1)S(1)}, u32[]{:S(2)}, u32[]{:S(2)}) collective-permute-start(bf16[8,2304]{1,0:T(8,128)(2,1)S(1)} %activate.1.rest_3_), channel_id=1, source_target_pairs={{0,2},{1,3},{2,0},{3,1},{4,6},{5,7},{6,4},{7,5},{8,10},{9,11},{10,... | collective-permute-start | bytes 110600 | tf_op jit(solution)/shard_map/ppermute | solution.py:704
  63.8 1.8 %collective-permute-start.16 = (bf16[8,2304]{1,0:T(8,128)(2,1)S(1)}, bf16[8,2304]{1,0:T(8,128)(2,1)S(1)}, u32[]{:S(2)}, u32[]{:S(2)}) collective-permute-start(bf16[8,2304]{1,0:T(8,128)(2,1)S(1)} %activate.1.rest_3_), channel_id=1, source_target_pairs={{0,3},{1,2},{2,1},{3,0},{4,7},{5,6},{6,5},{7,4},{8,11},{9,10},{10,... | collective-permute-start | bytes 110600 | tf_op jit(solution)/shard_map/ppermute | solution.py:704
  65.9 2.4 %collective-permute-done.15.rest_0_ = bf16[8,2304]{1,0:T(8,128)(2,1)S(1)} collective-permute-done((bf16[8,2304]{1,0:T(8,128)(2,1)S(1)}, bf16[8,2304]{1,0:T(8,128)(2,1)S(1)}, u32[]{:S(2)}, u32[]{:S(2)}) %collective-permute-start.15) | collective-permute-done | bytes 36896 | tf_op jit(solution)/shard_map/ppermute | solution.py:704
  68.3 1.4 %collective-permute-done.16.rest_1_ = bf16[8,2304]{1,0:T(8,128)(2,1)S(1)} collective-permute-done((bf16[8,2304]{1,0:T(8,128)(2,1)S(1)}, bf16[8,2304]{1,0:T(8,128)(2,1)S(1)}, u32[]{:S(2)}, u32[]{:S(2)}) %collective-permute-start.16) | collective-permute-done | bytes 36896 | tf_op jit(solution)/shard_map/ppermute | solution.py:704
  73.0 1.3 %collective-permute-start.20 = (bf16[32,896]{1,0:T(8,128)(2,1)S(1)}, bf16[32,896]{1,0:T(8,128)(2,1)S(1)}, u32[]{:S(2)}, u32[]{:S(2)}) collective-permute-start(bf16[32,896]{1,0:T(8,128)(2,1)S(1)} %add_pair.3.rest_0_), channel_id=1, source_target_pairs={{0,16},{4,20},{8,24},{12,28},{16,0},{20,4},{24,8},{28,12},{1,17},{... | collective-permute-start | bytes 172040 | tf_op jit(solution)/shard_map/ppermute | solution.py:704
  74.2 1.4 %collective-permute-start.21 = (bf16[32,896]{1,0:T(8,128)(2,1)S(1)}, bf16[32,896]{1,0:T(8,128)(2,1)S(1)}, u32[]{:S(2)}, u32[]{:S(2)}) collective-permute-start(bf16[32,896]{1,0:T(8,128)(2,1)S(1)} %add_pair.3.rest_0_), channel_id=1, source_target_pairs={{0,24},{4,28},{8,16},{12,20},{16,8},{20,12},{24,0},{28,4},{1,25},{... | collective-permute-start | bytes 172040 | tf_op jit(solution)/shard_map/ppermute | solution.py:704
  77.1 2.2 %collective-permute-done.21.rest_3_ = bf16[32,896]{1,0:T(8,128)(2,1)S(1)} collective-permute-done((bf16[32,896]{1,0:T(8,128)(2,1)S(1)}, bf16[32,896]{1,0:T(8,128)(2,1)S(1)}, u32[]{:S(2)}, u32[]{:S(2)}) %collective-permute-start.21) | collective-permute-done | bytes 57376 | tf_op jit(solution)/shard_map/ppermute | solution.py:704
  79.4 1.2 %collective-permute-done.22.sibling_ref = bf16[32,896]{1,0:T(8,128)(2,1)S(1)} collective-permute-done((bf16[32,896]{1,0:T(8,128)(2,1)S(1)}, bf16[32,896]{1,0:T(8,128)(2,1)S(1)}, u32[]{:S(2)}, u32[]{:S(2)}) %collective-permute-start.22) | collective-permute-done | bytes 57376 | tf_op jit(solution)/shard_map/ppermute | solution.py:704
  (47 shorter events, 15.3 us)
Async XLA Ops:
  16.8 2.1 %collective-permute-start = (bf16[528,512]{1,0:T(8,128)(2,1)S(1)}, bf16[528,512]{1,0:T(8,128)(2,1)S(1)}, u32[]{:S(2)}, u32[]{:S(2)}) collective-permute-start(bf16[528,512]{1,0:T(8,128)(2,1)S(1)} %get-tuple-element.28), channel_id=1, source_target_pairs={{0,4},{4,0},{8,12},{12,8},{16,20},{20,16},{24,28},{28,24},{1,5},{5... | collective-permute-start | bytes 1622024 | tf_op jit(solution)/shard_map/ppermute | solution.py:704
  19.3 8.6 %collective-permute-start.1 = (bf16[144,512]{1,0:T(8,128)(2,1)S(1)}, bf16[144,512]{1,0:T(8,128)(2,1)S(1)}, u32[]{:S(2)}, u32[]{:S(2)}) collective-permute-start(bf16[144,512]{1,0:T(8,128)(2,1)S(1)} %get-tuple-element.29), channel_id=1, source_target_pairs={{0,24},{4,28},{8,16},{12,20},{16,8},{20,12},{24,0},{28,4},{1,25},{... | collective-permute-start | bytes 442376 | tf_op jit(solution)/shard_map/ppermute | solution.py:704
  23.2 7.5 %collective-permute-start.2 = (bf16[144,512]{1,0:T(8,128)(2,1)S(1)}, bf16[144,512]{1,0:T(8,128)(2,1)S(1)}, u32[]{:S(2)}, u32[]{:S(2)}) collective-permute-start(bf16[144,512]{1,0:T(8,128)(2,1)S(1)} %get-tuple-element.30), channel_id=1, source_target_pairs={{0,16},{4,20},{8,24},{12,28},{16,0},{20,4},{24,8},{28,12},{1,17},{... | collective-permute-start | bytes 442376 | tf_op jit(solution)/shard_map/ppermute | solution.py:704
  23.7 7.1 %collective-permute-start.3 = (bf16[144,512]{1,0:T(8,128)(2,1)S(1)}, bf16[144,512]{1,0:T(8,128)(2,1)S(1)}, u32[]{:S(2)}, u32[]{:S(2)}) collective-permute-start(bf16[144,512]{1,0:T(8,128)(2,1)S(1)} %get-tuple-element.31), channel_id=1, source_target_pairs={{0,8},{4,12},{8,0},{12,4},{16,24},{20,28},{24,16},{28,20},{1,9},{5... | collective-permute-start | bytes 442376 | tf_op jit(solution)/shard_map/ppermute | solution.py:704
  31.5 5.2 %collective-permute-start.4 = (bf16[8,2048]{1,0:T(8,128)(2,1)S(1)}, bf16[8,2048]{1,0:T(8,128)(2,1)S(1)}, u32[]{:S(2)}, u32[]{:S(2)}) collective-permute-start(bf16[8,2048]{1,0:T(8,128)(2,1)S(1)} %merge_values.1.rest_3_), channel_id=1, source_target_pairs={{0,2},{1,3},{2,0},{3,1},{4,6},{5,7},{6,4},{7,5},{8,10},{9,11},{10,... | collective-permute-start | bytes 98312 | tf_op jit(solution)/shard_map/ppermute | solution.py:704
  34.0 5.8 %collective-permute-start.5 = (bf16[8,2048]{1,0:T(8,128)(2,1)S(1)}, bf16[8,2048]{1,0:T(8,128)(2,1)S(1)}, u32[]{:S(2)}, u32[]{:S(2)}) collective-permute-start(bf16[8,2048]{1,0:T(8,128)(2,1)S(1)} %merge_values.1.rest_3_), channel_id=1, source_target_pairs={{0,3},{1,2},{2,1},{3,0},{4,7},{5,6},{6,5},{7,4},{8,11},{9,10},{10,... | collective-permute-start | bytes 98312 | tf_op jit(solution)/shard_map/ppermute | solution.py:704
  35.7 4.3 %collective-permute-start.6 = (bf16[8,2048]{1,0:T(8,128)(2,1)S(1)}, bf16[8,2048]{1,0:T(8,128)(2,1)S(1)}, u32[]{:S(2)}, u32[]{:S(2)}) collective-permute-start(bf16[8,2048]{1,0:T(8,128)(2,1)S(1)} %merge_values.1.rest_3_), channel_id=1, source_target_pairs={{0,1},{1,0},{2,3},{3,2},{4,5},{5,4},{6,7},{7,6},{8,9},{9,8},{10,11... | collective-permute-start | bytes 98312 | tf_op jit(solution)/shard_map/ppermute | solution.py:704
  40.7 1.3 %collective-permute-start.7 = (bf16[32,896]{1,0:T(8,128)(2,1)S(1)}, bf16[32,896]{1,0:T(8,128)(2,1)S(1)}, u32[]{:S(2)}, u32[]{:S(2)}) collective-permute-start(bf16[32,896]{1,0:T(8,128)(2,1)S(1)} %get-tuple-element.34), channel_id=1, source_target_pairs={{0,4},{4,0},{8,12},{12,8},{16,20},{20,16},{24,28},{28,24},{1,5},{5... | collective-permute-start | bytes 172040 | tf_op jit(solution)/shard_map/ppermute | solution.py:704
  42.0 5.7 %collective-permute-start.10 = (bf16[32,896]{1,0:T(8,128)(2,1)S(1)}, bf16[32,896]{1,0:T(8,128)(2,1)S(1)}, u32[]{:S(2)}, u32[]{:S(2)}) collective-permute-start(bf16[32,896]{1,0:T(8,128)(2,1)S(1)} %add_pair.2.rest_0_), channel_id=1, source_target_pairs={{0,24},{4,28},{8,16},{12,20},{16,8},{20,12},{24,0},{28,4},{1,25},{... | collective-permute-start | bytes 172040 | tf_op jit(solution)/shard_map/ppermute | solution.py:704
  43.6 4.3 %collective-permute-start.8 = (bf16[32,896]{1,0:T(8,128)(2,1)S(1)}, bf16[32,896]{1,0:T(8,128)(2,1)S(1)}, u32[]{:S(2)}, u32[]{:S(2)}) collective-permute-start(bf16[32,896]{1,0:T(8,128)(2,1)S(1)} %add_pair.2.rest_0_), channel_id=1, source_target_pairs={{0,8},{4,12},{8,0},{12,4},{16,24},{20,28},{24,16},{28,20},{1,9},{5... | collective-permute-start | bytes 172040 | tf_op jit(solution)/shard_map/ppermute | solution.py:704
  44.6 4.2 %collective-permute-start.9 = (bf16[32,896]{1,0:T(8,128)(2,1)S(1)}, bf16[32,896]{1,0:T(8,128)(2,1)S(1)}, u32[]{:S(2)}, u32[]{:S(2)}) collective-permute-start(bf16[32,896]{1,0:T(8,128)(2,1)S(1)} %add_pair.2.rest_0_), channel_id=1, source_target_pairs={{0,16},{4,20},{8,24},{12,28},{16,0},{20,4},{24,8},{28,12},{1,17},{... | collective-permute-start | bytes 172040 | tf_op jit(solution)/shard_map/ppermute | solution.py:704
  48.8 1.7 %collective-permute-start.11 = (bf16[32,896]{1,0:T(8,128)(2,1)S(1)}, bf16[32,896]{1,0:T(8,128)(2,1)S(1)}, u32[]{:S(2)}, u32[]{:S(2)}) collective-permute-start(bf16[32,896]{1,0:T(8,128)(2,1)S(1)} %project_out_sum.1.mine_ref.base_ref), channel_id=1, source_target_pairs={{0,4},{4,0},{8,12},{12,8},{16,20},{20,16},{24,28},{28,24},{1,5},{5... | collective-permute-start | bytes 172040 | tf_op jit(solution)/shard_map/ppermute | solution.py:704
  48.9 21.0 %slice-start = ((s8[8257536]{0:T(1024)(128)(4,1)}), s8[4194304]{0:T(1024)(128)(4,1)S(1)}, s32[]{:S(2)}) async-start(s8[8257536]{0:T(1024)(128)(4,1)} %bitcast.2), calls=%async_computation | async-start | bytes 8388608
  52.1 8.8 %collective-permute-start.12 = (bf16[8,4736]{1,0:T(8,128)(2,1)S(1)}, bf16[8,4736]{1,0:T(8,128)(2,1)S(1)}, u32[]{:S(2)}, u32[]{:S(2)}) collective-permute-start(bf16[8,4736]{1,0:T(8,128)(2,1)S(1)} %get-tuple-element.39), channel_id=1, source_target_pairs={{0,2},{1,3},{2,0},{3,1},{4,6},{5,7},{6,4},{7,5},{8,10},{9,11},{10,... | collective-permute-start | bytes 227336 | tf_op jit(solution)/shard_map/ppermute | solution.py:704
  53.8 7.0 %collective-permute-start.13 = (bf16[8,4736]{1,0:T(8,128)(2,1)S(1)}, bf16[8,4736]{1,0:T(8,128)(2,1)S(1)}, u32[]{:S(2)}, u32[]{:S(2)}) collective-permute-start(bf16[8,4736]{1,0:T(8,128)(2,1)S(1)} %get-tuple-element.40), channel_id=1, source_target_pairs={{0,3},{1,2},{2,1},{3,0},{4,7},{5,6},{6,5},{7,4},{8,11},{9,10},{10,... | collective-permute-start | bytes 227336 | tf_op jit(solution)/shard_map/ppermute | solution.py:704
  54.8 7.3 %collective-permute-start.14 = (bf16[8,4736]{1,0:T(8,128)(2,1)S(1)}, bf16[8,4736]{1,0:T(8,128)(2,1)S(1)}, u32[]{:S(2)}, u32[]{:S(2)}) collective-permute-start(bf16[8,4736]{1,0:T(8,128)(2,1)S(1)} %get-tuple-element.41), channel_id=1, source_target_pairs={{0,1},{1,0},{2,3},{3,2},{4,5},{5,4},{6,7},{7,6},{8,9},{9,8},{10,11... | collective-permute-start | bytes 227336 | tf_op jit(solution)/shard_map/ppermute | solution.py:704
  62.3 6.0 %collective-permute-start.15 = (bf16[8,2304]{1,0:T(8,128)(2,1)S(1)}, bf16[8,2304]{1,0:T(8,128)(2,1)S(1)}, u32[]{:S(2)}, u32[]{:S(2)}) collective-permute-start(bf16[8,2304]{1,0:T(8,128)(2,1)S(1)} %activate.1.rest_3_), channel_id=1, source_target_pairs={{0,2},{1,3},{2,0},{3,1},{4,6},{5,7},{6,4},{7,5},{8,10},{9,11},{10,... | collective-permute-start | bytes 110600 | tf_op jit(solution)/shard_map/ppermute | solution.py:704
  63.8 5.9 %collective-permute-start.16 = (bf16[8,2304]{1,0:T(8,128)(2,1)S(1)}, bf16[8,2304]{1,0:T(8,128)(2,1)S(1)}, u32[]{:S(2)}, u32[]{:S(2)}) collective-permute-start(bf16[8,2304]{1,0:T(8,128)(2,1)S(1)} %activate.1.rest_3_), channel_id=1, source_target_pairs={{0,3},{1,2},{2,1},{3,0},{4,7},{5,6},{6,5},{7,4},{8,11},{9,10},{10,... | collective-permute-start | bytes 110600 | tf_op jit(solution)/shard_map/ppermute | solution.py:704
  65.6 4.4 %collective-permute-start.17 = (bf16[8,2304]{1,0:T(8,128)(2,1)S(1)}, bf16[8,2304]{1,0:T(8,128)(2,1)S(1)}, u32[]{:S(2)}, u32[]{:S(2)}) collective-permute-start(bf16[8,2304]{1,0:T(8,128)(2,1)S(1)} %activate.1.rest_3_), channel_id=1, source_target_pairs={{0,1},{1,0},{2,3},{3,2},{4,5},{5,4},{6,7},{7,6},{8,9},{9,8},{10,11... | collective-permute-start | bytes 110600 | tf_op jit(solution)/shard_map/ppermute | solution.py:704
  70.8 1.3 %collective-permute-start.18 = (bf16[32,896]{1,0:T(8,128)(2,1)S(1)}, bf16[32,896]{1,0:T(8,128)(2,1)S(1)}, u32[]{:S(2)}, u32[]{:S(2)}) collective-permute-start(bf16[32,896]{1,0:T(8,128)(2,1)S(1)} %get-tuple-element.44), channel_id=1, source_target_pairs={{0,4},{4,0},{8,12},{12,8},{16,20},{20,16},{24,28},{28,24},{1,5},{5... | collective-permute-start | bytes 172040 | tf_op jit(solution)/shard_map/ppermute | solution.py:704
  72.1 4.2 %collective-permute-start.19 = (bf16[32,896]{1,0:T(8,128)(2,1)S(1)}, bf16[32,896]{1,0:T(8,128)(2,1)S(1)}, u32[]{:S(2)}, u32[]{:S(2)}) collective-permute-start(bf16[32,896]{1,0:T(8,128)(2,1)S(1)} %add_pair.3.rest_0_), channel_id=1, source_target_pairs={{0,8},{4,12},{8,0},{12,4},{16,24},{20,28},{24,16},{28,20},{1,9},{5... | collective-permute-start | bytes 172040 | tf_op jit(solution)/shard_map/ppermute | solution.py:704
  73.0 4.2 %collective-permute-start.20 = (bf16[32,896]{1,0:T(8,128)(2,1)S(1)}, bf16[32,896]{1,0:T(8,128)(2,1)S(1)}, u32[]{:S(2)}, u32[]{:S(2)}) collective-permute-start(bf16[32,896]{1,0:T(8,128)(2,1)S(1)} %add_pair.3.rest_0_), channel_id=1, source_target_pairs={{0,16},{4,20},{8,24},{12,28},{16,0},{20,4},{24,8},{28,12},{1,17},{... | collective-permute-start | bytes 172040 | tf_op jit(solution)/shard_map/ppermute | solution.py:704
  74.2 5.1 %collective-permute-start.21 = (bf16[32,896]{1,0:T(8,128)(2,1)S(1)}, bf16[32,896]{1,0:T(8,128)(2,1)S(1)}, u32[]{:S(2)}, u32[]{:S(2)}) collective-permute-start(bf16[32,896]{1,0:T(8,128)(2,1)S(1)} %add_pair.3.rest_0_), channel_id=1, source_target_pairs={{0,24},{4,28},{8,16},{12,20},{16,8},{20,12},{24,0},{28,4},{1,25},{... | collective-permute-start | bytes 172040 | tf_op jit(solution)/shard_map/ppermute | solution.py:704
  79.4 1.3 %collective-permute-start.22 = (bf16[32,896]{1,0:T(8,128)(2,1)S(1)}, bf16[32,896]{1,0:T(8,128)(2,1)S(1)}, u32[]{:S(2)}, u32[]{:S(2)}) collective-permute-start(bf16[32,896]{1,0:T(8,128)(2,1)S(1)} %project_down_sum.1.mine_ref), channel_id=1, source_target_pairs={{0,4},{4,0},{8,12},{12,8},{16,20},{20,16},{24,28},{28,24},{1,5},{5... | collective-permute-start | bytes 172040 | tf_op jit(solution)/shard_map/ppermute | solution.py:704
  (3 other events, 54.2 us)

commit v2 on v1

--- a/solution.py
+++ b/solution.py
@@ -219,6 +219,19 @@
     me = lax.axis_index("kv")
     core = lax.rem(me, 2)
 
+    query_copy = pltpu.make_async_copy(query_hbm, query_t, query_sem)
+    query_copy.start()
+
+    def key_copy(s, j):
+        cols = pl.ds(pl.multiple_of(j * pair, pair), pair)
+        return pltpu.make_async_copy(key_hbm.at[s, :, cols], keys.at[s, :, cols], key_sem.at[s, j])
+
+    later_copies = [key_copy(s, j) for s in range(seqs) for j in range(pair_total)]
+    later_copies.pop(0).start()
+    weight_copies = [
+        pltpu.make_async_copy(weights_hbm[w], weights_ref[w], weight_sem.at[w]) for w in range(weight_count)
+    ]
+
     row_of = []
     for s in range(seqs):
         found = jnp.int32(0)
@@ -229,44 +242,18 @@
             found = found + mine.astype(jnp.int32)
         row_of.append(slots)
 
-    def key_copy(s, c):
-        cols = pl.ds(pl.multiple_of(c * CHUNK, CHUNK), CHUNK)
-        return pltpu.make_async_copy(key_hbm.at[s, :, cols], keys.at[s, :, cols], key_sem.at[s, c])
-
-    def query_copy(s, i):
-        return pltpu.make_async_copy(
-            query_hbm.at[row_of[s][i]], query_t.at[s * steps + i], query_sem.at[s, i]
-        )
-
-    for i in range(steps):
-        query_copy(0, i).start()
-    later_copies = [key_copy(s, c) for s in range(seqs) for c in range(2 * pair_total)]
-    later_copies.pop(0).start()
-    later_copies += [query_copy(s, i) for s in range(1, seqs) for i in range(steps)]
-    weight_copies = [
-        pltpu.make_async_copy(weights_hbm[w], weights_ref[w], weight_sem.at[w]) for w in range(weight_count)
-    ]
-
-    def turn_queries(s, meanwhile=()):
+    query_copy.wait()
+    for copy in later_copies:
+        copy.start()
+    for s in range(seqs):
         for i in range(steps):
-            query_copy(s, i).wait()
-        for copy in meanwhile:
-            copy.start()
-        for i in range(steps):
-            query_s[s, i * head_count : (i + 1) * head_count, :] = query_t[s * steps + i].T
-
-    turn_queries(0, later_copies[:1])
-    for copy in later_copies[1:]:
-        copy.start()
-    weight_start = [(0, pair_total - 1) if w < 2 else (seqs - 1, 0) for w in range(weight_count)]
+            query_s[s, i * head_count : (i + 1) * head_count, :] = query_t[row_of[s][i]].T
 
     row_iota = lax.broadcasted_iota(jnp.int32, (rows_in, 128), 0)
     owner = me == kv_count - 1
     logs[...] = jnp.zeros_like(logs)
 
     for s in range(seqs):
-        if s > 0:
-            turn_queries(s)
 
         @pl.when(jnp.logical_not(owner))
         def start_empty():
@@ -299,12 +286,9 @@
         live = jnp.clip(len_ref[s] - me * ctx, 0, ctx)
         live_pairs = lax.div(live + (pair - 1), pair)
 
-        def add_pair_of_chunks(base, masked):
+        def add_block(base, masked):
             halves = [pl.ds(base, CHUNK), pl.ds(base + CHUNK, CHUNK)]
-            scores = []
-            for h in range(2):
-                key_copy(s, lax.div(base, CHUNK) + h).wait()
-                scores.append(dot_f32(query_s[s], keys[s, :, halves[h]]))
+            scores = [dot_f32(query_s[s], keys[s, :, half]) for half in halves]
             for h in range(2):
                 score = scores[h]
                 if masked:
@@ -323,37 +307,37 @@
                 acc[...] = acc[...] * jnp.concatenate([scale] * (lat // 128), axis=1) + update
 
         def visit(j, carry):
-            for copy, (at_seq, at_block) in zip(weight_copies, weight_start):
-                if at_seq == s:
-                    @pl.when(j == at_block)
-                    def start_weight(copy=copy):
-                        copy.start()
+            key_copy(s, j).wait()
+            if s == 0:
+                for w in range(weight_count):
+                    @pl.when(j == w % pair_total)
+                    def start_weight():
+                        weight_copies[w].start()
             base = pl.multiple_of(j * pair, pair)
             whole = base + pair <= live
 
             @pl.when(whole)
             def all_live():
-                add_pair_of_chunks(base, False)
+                add_block(base, False)
 
             @pl.when(jnp.logical_not(whole))
             def some_live():
-                add_pair_of_chunks(base, True)
+                add_block(base, True)
 
             return carry
 
         lax.fori_loop(0, live_pairs, visit, 0)
 
         def skip(j, carry):
-            key_copy(s, 2 * j).wait()
-            key_copy(s, 2 * j + 1).wait()
+            key_copy(s, j).wait()
             return carry
 
         lax.fori_loop(live_pairs, pair_total, skip, 0)
-        for copy, (at_seq, at_block) in zip(weight_copies, weight_start):
-            if at_seq == s:
-                @pl.when(live_pairs <= at_block)
-                def start_weight(copy=copy):
-                    copy.start()
+        if s == 0:
+            for w in range(weight_count):
+                @pl.when(live_pairs <= w % pair_total)
+                def start_weight():
+                    weight_copies[w].start()
 
         total = jnp.sum(row_sum[...], axis=1, keepdims=True)
         some = total > 0.0
@@ -398,8 +382,8 @@
             pltpu.VMEM((group, 128), F32),
             pltpu.VMEM((group, 128), F32),
             pltpu.VMEM((rows_in, 128), F32),
-            pltpu.SemaphoreType.DMA((seqs, rows_in // seqs)),
-            pltpu.SemaphoreType.DMA((seqs, ctx // CHUNK)),
+            pltpu.SemaphoreType.DMA,
+            pltpu.SemaphoreType.DMA((seqs, ctx // (2 * CHUNK))),
             pltpu.SemaphoreType.DMA((len(weights),)),
         ],
         compiler_params=pltpu.CompilerParams(vmem_limit_bytes=26 * MIB),

time: 81.5 us -> 81 us (level)
  transfers between devices with their start and end apart: 23 -> 23, of which waited for: 20 -> 19; matrix products, arithmetic and copies ran while one was open for 0% -> 0% of each run, Pallas kernels for 4% -> 4%
where the time goes in v2:
time: 81 us; the launch traced here: 80.8 us
  waiting for transfers between devices  32.4 us (40%)
  Pallas kernels  24.3 us (30%)
  starting transfers between devices  23.8 us (29%)
    ppermute x23, waiting for transfers between devices, partner(): return lax.ppermute(array, axis, pairs)  32.4 us
    ppermute x23, starting transfers between devices, partner(): return lax.ppermute(array, axis, pairs)  23.8 us
    pallas_call x1, Pallas kernels, attention(): pl.pallas_call(functools.partial(attention_kernel, kv_count, len(weights)...  16.2 us
  transfers between devices with their start and end apart: 23, of which 19 were waited for; matrix products, arithmetic and copies ran while one was open for 0% of the time, Pallas kernels for 4%

profile of v2, /device:TPU:0, one launch (start us, length us, event | category | flops | bytes accessed | tf_op | source)
XLA Modules:
  0.0 80.8 jit_solution(17848925784207988419)
XLA Ops:
  0.0 16.2 %attention.1 = (bf16[528,512]{1,0:T(8,128)(2,1)S(1)}, bf16[528,512]{1,0:T(8,128)(2,1)S(1)}, bf16[16,512,128]{2,1,0:T(8,128)(2,1)S(1)}, bf16[2048,1792]{1,0:T(8,1...) custom-call(s32[2]{0:T(128)} %len_ref.1, s32[8]{0:T(128)} %seq_ref.1, s32[8]{0:T(128)} %pos_ref.1, ...), custom_call_target="tpu_custom_call" | custom-call | flops 9126805504 | bytes 9437184 | tf_op jit(solution)/shard_map/attention/pallas_call | solution.py:372
  16.7 1.6 %collective-permute-done.sibling_ref = bf16[528,512]{1,0:T(8,128)(2,1)S(1)} collective-permute-done((bf16[528,512]{1,0:T(8,128)(2,1)S(1)}, bf16[528,512]{1,0:T(8,128)(2,1)S(1)}, u32[]{:S(2)}, u32[]{:S(2)}) %collective-permute-start) | collective-permute-done | bytes 540704 | tf_op jit(solution)/shard_map/ppermute | solution.py:688
  18.7 3.9 %collective-permute-start.1 = (bf16[144,512]{1,0:T(8,128)(2,1)S(1)}, bf16[144,512]{1,0:T(8,128)(2,1)S(1)}, u32[]{:S(2)}, u32[]{:S(2)}) collective-permute-start(bf16[144,512]{1,0:T(8,128)(2,1)S(1)} %get-tuple-element.29), channel_id=1, source_target_pairs={{0,24},{4,28},{8,16},{12,20},{16,8},{20,12},{24,0},{28,4},{1,25},{... | collective-permute-start | bytes 442376 | tf_op jit(solution)/shard_map/ppermute | solution.py:688
  23.2 4.0 %collective-permute-done.1.rest_0_ = bf16[144,512]{1,0:T(8,128)(2,1)S(1)} collective-permute-done((bf16[144,512]{1,0:T(8,128)(2,1)S(1)}, bf16[144,512]{1,0:T(8,128)(2,1)S(1)}, u32[]{:S(2)}, u32[]{:S(2)}) %collective-permute-start.1) | collective-permute-done | bytes 147488 | tf_op jit(solution)/shard_map/ppermute | solution.py:688
  27.2 2.7 %collective-permute-done.2.rest_1_ = bf16[144,512]{1,0:T(8,128)(2,1)S(1)} collective-permute-done((bf16[144,512]{1,0:T(8,128)(2,1)S(1)}, bf16[144,512]{1,0:T(8,128)(2,1)S(1)}, u32[]{:S(2)}, u32[]{:S(2)}) %collective-permute-start.2) | collective-permute-done | bytes 147488 | tf_op jit(solution)/shard_map/ppermute | solution.py:688
  30.9 2.8 %collective-permute-start.4 = (bf16[8,2048]{1,0:T(8,128)(2,1)S(1)}, bf16[8,2048]{1,0:T(8,128)(2,1)S(1)}, u32[]{:S(2)}, u32[]{:S(2)}) collective-permute-start(bf16[8,2048]{1,0:T(8,128)(2,1)S(1)} %merge_values.1.rest_3_), channel_id=1, source_target_pairs={{0,2},{1,3},{2,0},{3,1},{4,6},{5,7},{6,4},{7,5},{8,10},{9,11},{10,... | collective-permute-start | bytes 98312 | tf_op jit(solution)/shard_map/ppermute | solution.py:688
  33.7 1.2 %collective-permute-start.5 = (bf16[8,2048]{1,0:T(8,128)(2,1)S(1)}, bf16[8,2048]{1,0:T(8,128)(2,1)S(1)}, u32[]{:S(2)}, u32[]{:S(2)}) collective-permute-start(bf16[8,2048]{1,0:T(8,128)(2,1)S(1)} %merge_values.1.rest_3_), channel_id=1, source_target_pairs={{0,3},{1,2},{2,1},{3,0},{4,7},{5,6},{6,5},{7,4},{8,11},{9,10},{10,... | collective-permute-start | bytes 98312 | tf_op jit(solution)/shard_map/ppermute | solution.py:688
  36.1 3.3 %collective-permute-done.5.rest_1_ = bf16[8,2048]{1,0:T(8,128)(2,1)S(1)} collective-permute-done((bf16[8,2048]{1,0:T(8,128)(2,1)S(1)}, bf16[8,2048]{1,0:T(8,128)(2,1)S(1)}, u32[]{:S(2)}, u32[]{:S(2)}) %collective-permute-start.5) | collective-permute-done | bytes 32800 | tf_op jit(solution)/shard_map/ppermute | solution.py:688
  41.4 1.4 %collective-permute-start.10 = (bf16[32,896]{1,0:T(8,128)(2,1)S(1)}, bf16[32,896]{1,0:T(8,128)(2,1)S(1)}, u32[]{:S(2)}, u32[]{:S(2)}) collective-permute-start(bf16[32,896]{1,0:T(8,128)(2,1)S(1)} %add_pair.2.rest_0_), channel_id=1, source_target_pairs={{0,24},{4,28},{8,16},{12,20},{16,8},{20,12},{24,0},{28,4},{1,25},{... | collective-permute-start | bytes 172040 | tf_op jit(solution)/shard_map/ppermute | solution.py:688
  42.8 1.6 %collective-permute-start.8 = (bf16[32,896]{1,0:T(8,128)(2,1)S(1)}, bf16[32,896]{1,0:T(8,128)(2,1)S(1)}, u32[]{:S(2)}, u32[]{:S(2)}) collective-permute-start(bf16[32,896]{1,0:T(8,128)(2,1)S(1)} %add_pair.2.rest_0_), channel_id=1, source_target_pairs={{0,8},{4,12},{8,0},{12,4},{16,24},{20,28},{24,16},{28,20},{1,9},{5... | collective-permute-start | bytes 172040 | tf_op jit(solution)/shard_map/ppermute | solution.py:688
  45.0 2.0 %collective-permute-done.10.rest_3_ = bf16[32,896]{1,0:T(8,128)(2,1)S(1)} collective-permute-done((bf16[32,896]{1,0:T(8,128)(2,1)S(1)}, bf16[32,896]{1,0:T(8,128)(2,1)S(1)}, u32[]{:S(2)}, u32[]{:S(2)}) %collective-permute-start.10) | collective-permute-done | bytes 57376 | tf_op jit(solution)/shard_map/ppermute | solution.py:688
  48.7 1.5 %gate_up_mine.1 = (f32[32,4608]{1,0:T(8,128)S(1)}, f32[32,128]{1,0:T(8,128)S(1)}) custom-call(bf16[1792,2304]{1,0:T(8,128)(2,1)S(1)} %get-tuple-element.35.gate_ref, bf16[1792,2304]{1,0:T(8,128)(2,1)S(1)} %get-tuple-element.36.up_ref, f32[1,1792]{1,0:T(1,128)S(1)} %reshape.3.gain_ref, bf16[32,896]{1,0:T(8,128)(2,1)S(1)} %project_out_sum.1.mine_ref.base_ref), custom_call_target="tpu_custom_call" | custom-call | flops 264241152 | bytes 8257536 | tf_op jit(solution)/shard_map/gate_up_mine/pallas_call | solution.py:618
  50.3 1.6 %gate_up_rest.1 = (bf16[8,4736]{1,0:T(8,128)(2,1)S(1)}, bf16[8,4736]{1,0:T(8,128)(2,1)S(1)}, bf16[8,4736]{1,0:T(8,128)(2,1)S(1)}, bf16[8,4736]{1,0:T(8,128)(2,1)S(1)}) custom-call(bf16[1792,2304]{1,0:T(8,128)(2,1)S(1)} %get-tuple-element.35.gate_ref, bf16[1792,2304]{1,0:T(8,128)(2,1)S(1)} %get-tuple-element.36.up_ref, f32[1,1792]{1,0:T(1,128)S(1)} %reshape.3.gain_ref, ...), custom_call_target="tpu_custom_call" | custom-call | flops 264241152 | bytes 8257536 | tf_op jit(solution)/shard_map/gate_up_rest/pallas_call | solution.py:631
  54.1 1.4 %collective-permute-start.14 = (bf16[8,4736]{1,0:T(8,128)(2,1)S(1)}, bf16[8,4736]{1,0:T(8,128)(2,1)S(1)}, u32[]{:S(2)}, u32[]{:S(2)}) collective-permute-start(bf16[8,4736]{1,0:T(8,128)(2,1)S(1)} %get-tuple-element.41), channel_id=1, source_target_pairs={{0,1},{1,0},{2,3},{3,2},{4,5},{5,4},{6,7},{7,6},{8,9},{9,8},{10,11... | collective-permute-start | bytes 227336 | tf_op jit(solution)/shard_map/ppermute | solution.py:688
  55.4 4.9 %collective-permute-done.12.rest_0_ = bf16[8,4736]{1,0:T(8,128)(2,1)S(1)} collective-permute-done((bf16[8,4736]{1,0:T(8,128)(2,1)S(1)}, bf16[8,4736]{1,0:T(8,128)(2,1)S(1)}, u32[]{:S(2)}, u32[]{:S(2)}) %collective-permute-start.12) | collective-permute-done | bytes 75808 | tf_op jit(solution)/shard_map/ppermute | solution.py:688
  60.3 1.3 %collective-permute-done.14.rest_2_ = bf16[8,4736]{1,0:T(8,128)(2,1)S(1)} collective-permute-done((bf16[8,4736]{1,0:T(8,128)(2,1)S(1)}, bf16[8,4736]{1,0:T(8,128)(2,1)S(1)}, u32[]{:S(2)}, u32[]{:S(2)}) %collective-permute-start.14) | collective-permute-done | bytes 75808 | tf_op jit(solution)/shard_map/ppermute | solution.py:688
  61.8 2.0 %collective-permute-start.15 = (bf16[8,2304]{1,0:T(8,128)(2,1)S(1)}, bf16[8,2304]{1,0:T(8,128)(2,1)S(1)}, u32[]{:S(2)}, u32[]{:S(2)}) collective-permute-start(bf16[8,2304]{1,0:T(8,128)(2,1)S(1)} %activate.1.rest_3_), channel_id=1, source_target_pairs={{0,2},{1,3},{2,0},{3,1},{4,6},{5,7},{6,4},{7,5},{8,10},{9,11},{10,... | collective-permute-start | bytes 110600 | tf_op jit(solution)/shard_map/ppermute | solution.py:688
  63.8 1.2 %collective-permute-start.16 = (bf16[8,2304]{1,0:T(8,128)(2,1)S(1)}, bf16[8,2304]{1,0:T(8,128)(2,1)S(1)}, u32[]{:S(2)}, u32[]{:S(2)}) collective-permute-start(bf16[8,2304]{1,0:T(8,128)(2,1)S(1)} %activate.1.rest_3_), channel_id=1, source_target_pairs={{0,3},{1,2},{2,1},{3,0},{4,7},{5,6},{6,5},{7,4},{8,11},{9,10},{10,... | collective-permute-start | bytes 110600 | tf_op jit(solution)/shard_map/ppermute | solution.py:688
  65.4 2.2 %collective-permute-done.15.rest_0_ = bf16[8,2304]{1,0:T(8,128)(2,1)S(1)} collective-permute-done((bf16[8,2304]{1,0:T(8,128)(2,1)S(1)}, bf16[8,2304]{1,0:T(8,128)(2,1)S(1)}, u32[]{:S(2)}, u32[]{:S(2)}) %collective-permute-start.15) | collective-permute-done | bytes 36896 | tf_op jit(solution)/shard_map/ppermute | solution.py:688
  67.6 2.0 %collective-permute-done.16.rest_1_ = bf16[8,2304]{1,0:T(8,128)(2,1)S(1)} collective-permute-done((bf16[8,2304]{1,0:T(8,128)(2,1)S(1)}, bf16[8,2304]{1,0:T(8,128)(2,1)S(1)}, u32[]{:S(2)}, u32[]{:S(2)}) %collective-permute-start.16) | collective-permute-done | bytes 36896 | tf_op jit(solution)/shard_map/ppermute | solution.py:688
  72.2 1.4 %collective-permute-start.20 = (bf16[32,896]{1,0:T(8,128)(2,1)S(1)}, bf16[32,896]{1,0:T(8,128)(2,1)S(1)}, u32[]{:S(2)}, u32[]{:S(2)}) collective-permute-start(bf16[32,896]{1,0:T(8,128)(2,1)S(1)} %add_pair.3.rest_0_), channel_id=1, source_target_pairs={{0,16},{4,20},{8,24},{12,28},{16,0},{20,4},{24,8},{28,12},{1,17},{... | collective-permute-start | bytes 172040 | tf_op jit(solution)/shard_map/ppermute | solution.py:688
  73.7 1.6 %collective-permute-start.21 = (bf16[32,896]{1,0:T(8,128)(2,1)S(1)}, bf16[32,896]{1,0:T(8,128)(2,1)S(1)}, u32[]{:S(2)}, u32[]{:S(2)}) collective-permute-start(bf16[32,896]{1,0:T(8,128)(2,1)S(1)} %add_pair.3.rest_0_), channel_id=1, source_target_pairs={{0,24},{4,28},{8,16},{12,20},{16,8},{20,12},{24,0},{28,4},{1,25},{... | collective-permute-start | bytes 172040 | tf_op jit(solution)/shard_map/ppermute | solution.py:688
  76.4 2.3 %collective-permute-done.21.rest_3_ = bf16[32,896]{1,0:T(8,128)(2,1)S(1)} collective-permute-done((bf16[32,896]{1,0:T(8,128)(2,1)S(1)}, bf16[32,896]{1,0:T(8,128)(2,1)S(1)}, u32[]{:S(2)}, u32[]{:S(2)}) %collective-permute-start.21) | collective-permute-done | bytes 57376 | tf_op jit(solution)/shard_map/ppermute | solution.py:688
  78.9 1.2 %collective-permute-done.22.sibling_ref = bf16[32,896]{1,0:T(8,128)(2,1)S(1)} collective-permute-done((bf16[32,896]{1,0:T(8,128)(2,1)S(1)}, bf16[32,896]{1,0:T(8,128)(2,1)S(1)}, u32[]{:S(2)}, u32[]{:S(2)}) %collective-permute-start.22) | collective-permute-done | bytes 57376 | tf_op jit(solution)/shard_map/ppermute | solution.py:688
  (47 shorter events, 15.3 us)
Async XLA Ops:
  16.2 2.1 %collective-permute-start = (bf16[528,512]{1,0:T(8,128)(2,1)S(1)}, bf16[528,512]{1,0:T(8,128)(2,1)S(1)}, u32[]{:S(2)}, u32[]{:S(2)}) collective-permute-start(bf16[528,512]{1,0:T(8,128)(2,1)S(1)} %get-tuple-element.28), channel_id=1, source_target_pairs={{0,4},{4,0},{8,12},{12,8},{16,20},{20,16},{24,28},{28,24},{1,5},{5... | collective-permute-start | bytes 1622024 | tf_op jit(solution)/shard_map/ppermute | solution.py:688
  18.7 8.5 %collective-permute-start.1 = (bf16[144,512]{1,0:T(8,128)(2,1)S(1)}, bf16[144,512]{1,0:T(8,128)(2,1)S(1)}, u32[]{:S(2)}, u32[]{:S(2)}) collective-permute-start(bf16[144,512]{1,0:T(8,128)(2,1)S(1)} %get-tuple-element.29), channel_id=1, source_target_pairs={{0,24},{4,28},{8,16},{12,20},{16,8},{20,12},{24,0},{28,4},{1,25},{... | collective-permute-start | bytes 442376 | tf_op jit(solution)/shard_map/ppermute | solution.py:688
  22.6 7.3 %collective-permute-start.2 = (bf16[144,512]{1,0:T(8,128)(2,1)S(1)}, bf16[144,512]{1,0:T(8,128)(2,1)S(1)}, u32[]{:S(2)}, u32[]{:S(2)}) collective-permute-start(bf16[144,512]{1,0:T(8,128)(2,1)S(1)} %get-tuple-element.30), channel_id=1, source_target_pairs={{0,16},{4,20},{8,24},{12,28},{16,0},{20,4},{24,8},{28,12},{1,17},{... | collective-permute-start | bytes 442376 | tf_op jit(solution)/shard_map/ppermute | solution.py:688
  23.1 7.1 %collective-permute-start.3 = (bf16[144,512]{1,0:T(8,128)(2,1)S(1)}, bf16[144,512]{1,0:T(8,128)(2,1)S(1)}, u32[]{:S(2)}, u32[]{:S(2)}) collective-permute-start(bf16[144,512]{1,0:T(8,128)(2,1)S(1)} %get-tuple-element.31), channel_id=1, source_target_pairs={{0,8},{4,12},{8,0},{12,4},{16,24},{20,28},{24,16},{28,20},{1,9},{5... | collective-permute-start | bytes 442376 | tf_op jit(solution)/shard_map/ppermute | solution.py:688
  30.9 5.2 %collective-permute-start.4 = (bf16[8,2048]{1,0:T(8,128)(2,1)S(1)}, bf16[8,2048]{1,0:T(8,128)(2,1)S(1)}, u32[]{:S(2)}, u32[]{:S(2)}) collective-permute-start(bf16[8,2048]{1,0:T(8,128)(2,1)S(1)} %merge_values.1.rest_3_), channel_id=1, source_target_pairs={{0,2},{1,3},{2,0},{3,1},{4,6},{5,7},{6,4},{7,5},{8,10},{9,11},{10,... | collective-permute-start | bytes 98312 | tf_op jit(solution)/shard_map/ppermute | solution.py:688
  33.7 5.7 %collective-permute-start.5 = (bf16[8,2048]{1,0:T(8,128)(2,1)S(1)}, bf16[8,2048]{1,0:T(8,128)(2,1)S(1)}, u32[]{:S(2)}, u32[]{:S(2)}) collective-permute-start(bf16[8,2048]{1,0:T(8,128)(2,1)S(1)} %merge_values.1.rest_3_), channel_id=1, source_target_pairs={{0,3},{1,2},{2,1},{3,0},{4,7},{5,6},{6,5},{7,4},{8,11},{9,10},{10,... | collective-permute-start | bytes 98312 | tf_op jit(solution)/shard_map/ppermute | solution.py:688
  34.9 4.5 %collective-permute-start.6 = (bf16[8,2048]{1,0:T(8,128)(2,1)S(1)}, bf16[8,2048]{1,0:T(8,128)(2,1)S(1)}, u32[]{:S(2)}, u32[]{:S(2)}) collective-permute-start(bf16[8,2048]{1,0:T(8,128)(2,1)S(1)} %merge_values.1.rest_3_), channel_id=1, source_target_pairs={{0,1},{1,0},{2,3},{3,2},{4,5},{5,4},{6,7},{7,6},{8,9},{9,8},{10,11... | collective-permute-start | bytes 98312 | tf_op jit(solution)/shard_map/ppermute | solution.py:688
  40.1 1.3 %collective-permute-start.7 = (bf16[32,896]{1,0:T(8,128)(2,1)S(1)}, bf16[32,896]{1,0:T(8,128)(2,1)S(1)}, u32[]{:S(2)}, u32[]{:S(2)}) collective-permute-start(bf16[32,896]{1,0:T(8,128)(2,1)S(1)} %get-tuple-element.34), channel_id=1, source_target_pairs={{0,4},{4,0},{8,12},{12,8},{16,20},{20,16},{24,28},{28,24},{1,5},{5... | collective-permute-start | bytes 172040 | tf_op jit(solution)/shard_map/ppermute | solution.py:688
  41.4 5.6 %collective-permute-start.10 = (bf16[32,896]{1,0:T(8,128)(2,1)S(1)}, bf16[32,896]{1,0:T(8,128)(2,1)S(1)}, u32[]{:S(2)}, u32[]{:S(2)}) collective-permute-start(bf16[32,896]{1,0:T(8,128)(2,1)S(1)} %add_pair.2.rest_0_), channel_id=1, source_target_pairs={{0,24},{4,28},{8,16},{12,20},{16,8},{20,12},{24,0},{28,4},{1,25},{... | collective-permute-start | bytes 172040 | tf_op jit(solution)/shard_map/ppermute | solution.py:688
  42.8 4.8 %collective-permute-start.8 = (bf16[32,896]{1,0:T(8,128)(2,1)S(1)}, bf16[32,896]{1,0:T(8,128)(2,1)S(1)}, u32[]{:S(2)}, u32[]{:S(2)}) collective-permute-start(bf16[32,896]{1,0:T(8,128)(2,1)S(1)} %add_pair.2.rest_0_), channel_id=1, source_target_pairs={{0,8},{4,12},{8,0},{12,4},{16,24},{20,28},{24,16},{28,20},{1,9},{5... | collective-permute-start | bytes 172040 | tf_op jit(solution)/shard_map/ppermute | solution.py:688
  44.4 4.2 %collective-permute-start.9 = (bf16[32,896]{1,0:T(8,128)(2,1)S(1)}, bf16[32,896]{1,0:T(8,128)(2,1)S(1)}, u32[]{:S(2)}, u32[]{:S(2)}) collective-permute-start(bf16[32,896]{1,0:T(8,128)(2,1)S(1)} %add_pair.2.rest_0_), channel_id=1, source_target_pairs={{0,16},{4,20},{8,24},{12,28},{16,0},{20,4},{24,8},{28,12},{1,17},{... | collective-permute-start | bytes 172040 | tf_op jit(solution)/shard_map/ppermute | solution.py:688
  48.6 1.7 %collective-permute-start.11 = (bf16[32,896]{1,0:T(8,128)(2,1)S(1)}, bf16[32,896]{1,0:T(8,128)(2,1)S(1)}, u32[]{:S(2)}, u32[]{:S(2)}) collective-permute-start(bf16[32,896]{1,0:T(8,128)(2,1)S(1)} %project_out_sum.1.mine_ref.base_ref), channel_id=1, source_target_pairs={{0,4},{4,0},{8,12},{12,8},{16,20},{20,16},{24,28},{28,24},{1,5},{5... | collective-permute-start | bytes 172040 | tf_op jit(solution)/shard_map/ppermute | solution.py:688
  48.7 20.8 %slice-start = ((s8[8257536]{0:T(1024)(128)(4,1)}), s8[4194304]{0:T(1024)(128)(4,1)S(1)}, s32[]{:S(2)}) async-start(s8[8257536]{0:T(1024)(128)(4,1)} %bitcast.2), calls=%async_computation | async-start | bytes 8388608
  51.9 8.4 %collective-permute-start.12 = (bf16[8,4736]{1,0:T(8,128)(2,1)S(1)}, bf16[8,4736]{1,0:T(8,128)(2,1)S(1)}, u32[]{:S(2)}, u32[]{:S(2)}) collective-permute-start(bf16[8,4736]{1,0:T(8,128)(2,1)S(1)} %get-tuple-element.39), channel_id=1, source_target_pairs={{0,2},{1,3},{2,0},{3,1},{4,6},{5,7},{6,4},{7,5},{8,10},{9,11},{10,... | collective-permute-start | bytes 227336 | tf_op jit(solution)/shard_map/ppermute | solution.py:688
  53.0 7.2 %collective-permute-start.13 = (bf16[8,4736]{1,0:T(8,128)(2,1)S(1)}, bf16[8,4736]{1,0:T(8,128)(2,1)S(1)}, u32[]{:S(2)}, u32[]{:S(2)}) collective-permute-start(bf16[8,4736]{1,0:T(8,128)(2,1)S(1)} %get-tuple-element.40), channel_id=1, source_target_pairs={{0,3},{1,2},{2,1},{3,0},{4,7},{5,6},{6,5},{7,4},{8,11},{9,10},{10,... | collective-permute-start | bytes 227336 | tf_op jit(solution)/shard_map/ppermute | solution.py:688
  54.1 7.6 %collective-permute-start.14 = (bf16[8,4736]{1,0:T(8,128)(2,1)S(1)}, bf16[8,4736]{1,0:T(8,128)(2,1)S(1)}, u32[]{:S(2)}, u32[]{:S(2)}) collective-permute-start(bf16[8,4736]{1,0:T(8,128)(2,1)S(1)} %get-tuple-element.41), channel_id=1, source_target_pairs={{0,1},{1,0},{2,3},{3,2},{4,5},{5,4},{6,7},{7,6},{8,9},{9,8},{10,11... | collective-permute-start | bytes 227336 | tf_op jit(solution)/shard_map/ppermute | solution.py:688
  61.8 5.8 %collective-permute-start.15 = (bf16[8,2304]{1,0:T(8,128)(2,1)S(1)}, bf16[8,2304]{1,0:T(8,128)(2,1)S(1)}, u32[]{:S(2)}, u32[]{:S(2)}) collective-permute-start(bf16[8,2304]{1,0:T(8,128)(2,1)S(1)} %activate.1.rest_3_), channel_id=1, source_target_pairs={{0,2},{1,3},{2,0},{3,1},{4,6},{5,7},{6,4},{7,5},{8,10},{9,11},{10,... | collective-permute-start | bytes 110600 | tf_op jit(solution)/shard_map/ppermute | solution.py:688
  63.8 5.8 %collective-permute-start.16 = (bf16[8,2304]{1,0:T(8,128)(2,1)S(1)}, bf16[8,2304]{1,0:T(8,128)(2,1)S(1)}, u32[]{:S(2)}, u32[]{:S(2)}) collective-permute-start(bf16[8,2304]{1,0:T(8,128)(2,1)S(1)} %activate.1.rest_3_), channel_id=1, source_target_pairs={{0,3},{1,2},{2,1},{3,0},{4,7},{5,6},{6,5},{7,4},{8,11},{9,10},{10,... | collective-permute-start | bytes 110600 | tf_op jit(solution)/shard_map/ppermute | solution.py:688
  65.0 4.5 %collective-permute-start.17 = (bf16[8,2304]{1,0:T(8,128)(2,1)S(1)}, bf16[8,2304]{1,0:T(8,128)(2,1)S(1)}, u32[]{:S(2)}, u32[]{:S(2)}) collective-permute-start(bf16[8,2304]{1,0:T(8,128)(2,1)S(1)} %activate.1.rest_3_), channel_id=1, source_target_pairs={{0,1},{1,0},{2,3},{3,2},{4,5},{5,4},{6,7},{7,6},{8,9},{9,8},{10,11... | collective-permute-start | bytes 110600 | tf_op jit(solution)/shard_map/ppermute | solution.py:688
  70.4 1.3 %collective-permute-start.18 = (bf16[32,896]{1,0:T(8,128)(2,1)S(1)}, bf16[32,896]{1,0:T(8,128)(2,1)S(1)}, u32[]{:S(2)}, u32[]{:S(2)}) collective-permute-start(bf16[32,896]{1,0:T(8,128)(2,1)S(1)} %get-tuple-element.44), channel_id=1, source_target_pairs={{0,4},{4,0},{8,12},{12,8},{16,20},{20,16},{24,28},{28,24},{1,5},{5... | collective-permute-start | bytes 172040 | tf_op jit(solution)/shard_map/ppermute | solution.py:688
  71.7 4.4 %collective-permute-start.19 = (bf16[32,896]{1,0:T(8,128)(2,1)S(1)}, bf16[32,896]{1,0:T(8,128)(2,1)S(1)}, u32[]{:S(2)}, u32[]{:S(2)}) collective-permute-start(bf16[32,896]{1,0:T(8,128)(2,1)S(1)} %add_pair.3.rest_0_), channel_id=1, source_target_pairs={{0,8},{4,12},{8,0},{12,4},{16,24},{20,28},{24,16},{28,20},{1,9},{5... | collective-permute-start | bytes 172040 | tf_op jit(solution)/shard_map/ppermute | solution.py:688
  72.2 4.2 %collective-permute-start.20 = (bf16[32,896]{1,0:T(8,128)(2,1)S(1)}, bf16[32,896]{1,0:T(8,128)(2,1)S(1)}, u32[]{:S(2)}, u32[]{:S(2)}) collective-permute-start(bf16[32,896]{1,0:T(8,128)(2,1)S(1)} %add_pair.3.rest_0_), channel_id=1, source_target_pairs={{0,16},{4,20},{8,24},{12,28},{16,0},{20,4},{24,8},{28,12},{1,17},{... | collective-permute-start | bytes 172040 | tf_op jit(solution)/shard_map/ppermute | solution.py:688
  73.7 5.1 %collective-permute-start.21 = (bf16[32,896]{1,0:T(8,128)(2,1)S(1)}, bf16[32,896]{1,0:T(8,128)(2,1)S(1)}, u32[]{:S(2)}, u32[]{:S(2)}) collective-permute-start(bf16[32,896]{1,0:T(8,128)(2,1)S(1)} %add_pair.3.rest_0_), channel_id=1, source_target_pairs={{0,24},{4,28},{8,16},{12,20},{16,8},{20,12},{24,0},{28,4},{1,25},{... | collective-permute-start | bytes 172040 | tf_op jit(solution)/shard_map/ppermute | solution.py:688
  78.8 1.3 %collective-permute-start.22 = (bf16[32,896]{1,0:T(8,128)(2,1)S(1)}, bf16[32,896]{1,0:T(8,128)(2,1)S(1)}, u32[]{:S(2)}, u32[]{:S(2)}) collective-permute-start(bf16[32,896]{1,0:T(8,128)(2,1)S(1)} %project_down_sum.1.mine_ref), channel_id=1, source_target_pairs={{0,4},{4,0},{8,12},{12,8},{16,20},{20,16},{24,28},{28,24},{1,5},{5... | collective-permute-start | bytes 172040 | tf_op jit(solution)/shard_map/ppermute | solution.py:688
  (3 other events, 54.8 us)

commit v3 on v2

--- a/solution.py
+++ b/solution.py
@@ -297,7 +297,7 @@
                 old_max = row_max[...]
                 new_max = jnp.maximum(old_max, jnp.max(score, axis=1, keepdims=True))
                 scale = jnp.exp2((old_max - new_max) * factor)
-                weight = jnp.exp2((score - jnp.concatenate([new_max] * (CHUNK // 128), axis=1)) * factor)
+                weight = jnp.exp2(score * factor - jnp.concatenate([new_max * factor] * (CHUNK // 128), axis=1))
                 part = weight[:, :128]
                 for c in range(1, CHUNK // 128):
                     part = part + weight[:, c * 128 : (c + 1) * 128]

time: 81 us -> 82.2 us (1.015)
  Pallas kernels: 24.3 us -> 25.6 us
    pallas_call x1, Pallas kernels: 16.2 us -> 17.4 us  [attention(): pl.pallas_call(functools.partial(attention_kernel, kv_count, len(weights)...]
where the time goes in v3:
time: 82.2 us; the launch traced here: 81.9 us
  waiting for transfers between devices  32.6 us (40%)
  Pallas kernels  25.6 us (31%)
  starting transfers between devices  23.6 us (29%)
    ppermute x23, waiting for transfers between devices, partner(): return lax.ppermute(array, axis, pairs)  32.6 us
    ppermute x23, starting transfers between devices, partner(): return lax.ppermute(array, axis, pairs)  23.6 us
    pallas_call x1, Pallas kernels, attention(): pl.pallas_call(functools.partial(attention_kernel, kv_count, len(weights)...  17.4 us
  transfers between devices with their start and end apart: 23, of which 19 were waited for; matrix products, arithmetic and copies ran while one was open for 0% of the time, Pallas kernels for 4%

profile of v3, /device:TPU:0, one launch (start us, length us, event | category | flops | bytes accessed | tf_op | source)
XLA Modules:
  0.0 81.9 jit_solution(15812054200700386144)
XLA Ops:
  0.0 17.4 %attention.1 = (bf16[528,512]{1,0:T(8,128)(2,1)S(1)}, bf16[528,512]{1,0:T(8,128)(2,1)S(1)}, bf16[16,512,128]{2,1,0:T(8,128)(2,1)S(1)}, bf16[2048,1792]{1,0:T(8,1...) custom-call(s32[2]{0:T(128)} %len_ref.1, s32[8]{0:T(128)} %seq_ref.1, s32[8]{0:T(128)} %pos_ref.1, ...), custom_call_target="tpu_custom_call" | custom-call | flops 9126805504 | bytes 9437184 | tf_op jit(solution)/shard_map/attention/pallas_call | solution.py:372
  18.0 1.6 %collective-permute-done.sibling_ref = bf16[528,512]{1,0:T(8,128)(2,1)S(1)} collective-permute-done((bf16[528,512]{1,0:T(8,128)(2,1)S(1)}, bf16[528,512]{1,0:T(8,128)(2,1)S(1)}, u32[]{:S(2)}, u32[]{:S(2)}) %collective-permute-start) | collective-permute-done | bytes 540704 | tf_op jit(solution)/shard_map/ppermute | solution.py:688
  20.1 4.3 %collective-permute-start.2 = (bf16[144,512]{1,0:T(8,128)(2,1)S(1)}, bf16[144,512]{1,0:T(8,128)(2,1)S(1)}, u32[]{:S(2)}, u32[]{:S(2)}) collective-permute-start(bf16[144,512]{1,0:T(8,128)(2,1)S(1)} %get-tuple-element.30), channel_id=1, source_target_pairs={{0,16},{4,20},{8,24},{12,28},{16,0},{20,4},{24,8},{28,12},{1,17},{... | collective-permute-start | bytes 442376 | tf_op jit(solution)/shard_map/ppermute | solution.py:688
  24.5 3.1 %collective-permute-done.1.rest_0_ = bf16[144,512]{1,0:T(8,128)(2,1)S(1)} collective-permute-done((bf16[144,512]{1,0:T(8,128)(2,1)S(1)}, bf16[144,512]{1,0:T(8,128)(2,1)S(1)}, u32[]{:S(2)}, u32[]{:S(2)}) %collective-permute-start.1) | collective-permute-done | bytes 147488 | tf_op jit(solution)/shard_map/ppermute | solution.py:688
  27.6 2.9 %collective-permute-done.2.rest_1_ = bf16[144,512]{1,0:T(8,128)(2,1)S(1)} collective-permute-done((bf16[144,512]{1,0:T(8,128)(2,1)S(1)}, bf16[144,512]{1,0:T(8,128)(2,1)S(1)}, u32[]{:S(2)}, u32[]{:S(2)}) %collective-permute-start.2) | collective-permute-done | bytes 147488 | tf_op jit(solution)/shard_map/ppermute | solution.py:688
  32.2 2.6 %collective-permute-start.4 = (bf16[8,2048]{1,0:T(8,128)(2,1)S(1)}, bf16[8,2048]{1,0:T(8,128)(2,1)S(1)}, u32[]{:S(2)}, u32[]{:S(2)}) collective-permute-start(bf16[8,2048]{1,0:T(8,128)(2,1)S(1)} %merge_values.1.rest_3_), channel_id=1, source_target_pairs={{0,2},{1,3},{2,0},{3,1},{4,6},{5,7},{6,4},{7,5},{8,10},{9,11},{10,... | collective-permute-start | bytes 98312 | tf_op jit(solution)/shard_map/ppermute | solution.py:688
  34.9 1.2 %collective-permute-start.5 = (bf16[8,2048]{1,0:T(8,128)(2,1)S(1)}, bf16[8,2048]{1,0:T(8,128)(2,1)S(1)}, u32[]{:S(2)}, u32[]{:S(2)}) collective-permute-start(bf16[8,2048]{1,0:T(8,128)(2,1)S(1)} %merge_values.1.rest_3_), channel_id=1, source_target_pairs={{0,3},{1,2},{2,1},{3,0},{4,7},{5,6},{6,5},{7,4},{8,11},{9,10},{10,... | collective-permute-start | bytes 98312 | tf_op jit(solution)/shard_map/ppermute | solution.py:688
  37.3 3.3 %collective-permute-done.5.rest_1_ = bf16[8,2048]{1,0:T(8,128)(2,1)S(1)} collective-permute-done((bf16[8,2048]{1,0:T(8,128)(2,1)S(1)}, bf16[8,2048]{1,0:T(8,128)(2,1)S(1)}, u32[]{:S(2)}, u32[]{:S(2)}) %collective-permute-start.5) | collective-permute-done | bytes 32800 | tf_op jit(solution)/shard_map/ppermute | solution.py:688
  42.7 1.5 %collective-permute-start.10 = (bf16[32,896]{1,0:T(8,128)(2,1)S(1)}, bf16[32,896]{1,0:T(8,128)(2,1)S(1)}, u32[]{:S(2)}, u32[]{:S(2)}) collective-permute-start(bf16[32,896]{1,0:T(8,128)(2,1)S(1)} %add_pair.2.rest_0_), channel_id=1, source_target_pairs={{0,24},{4,28},{8,16},{12,20},{16,8},{20,12},{24,0},{28,4},{1,25},{... | collective-permute-start | bytes 172040 | tf_op jit(solution)/shard_map/ppermute | solution.py:688
  44.2 1.5 %collective-permute-start.8 = (bf16[32,896]{1,0:T(8,128)(2,1)S(1)}, bf16[32,896]{1,0:T(8,128)(2,1)S(1)}, u32[]{:S(2)}, u32[]{:S(2)}) collective-permute-start(bf16[32,896]{1,0:T(8,128)(2,1)S(1)} %add_pair.2.rest_0_), channel_id=1, source_target_pairs={{0,8},{4,12},{8,0},{12,4},{16,24},{20,28},{24,16},{28,20},{1,9},{5... | collective-permute-start | bytes 172040 | tf_op jit(solution)/shard_map/ppermute | solution.py:688
  46.2 1.9 %collective-permute-done.10.rest_3_ = bf16[32,896]{1,0:T(8,128)(2,1)S(1)} collective-permute-done((bf16[32,896]{1,0:T(8,128)(2,1)S(1)}, bf16[32,896]{1,0:T(8,128)(2,1)S(1)}, u32[]{:S(2)}, u32[]{:S(2)}) %collective-permute-start.10) | collective-permute-done | bytes 57376 | tf_op jit(solution)/shard_map/ppermute | solution.py:688
  50.0 1.5 %gate_up_mine.1 = (f32[32,4608]{1,0:T(8,128)S(1)}, f32[32,128]{1,0:T(8,128)S(1)}) custom-call(bf16[1792,2304]{1,0:T(8,128)(2,1)S(1)} %get-tuple-element.35.gate_ref, bf16[1792,2304]{1,0:T(8,128)(2,1)S(1)} %get-tuple-element.36.up_ref, f32[1,1792]{1,0:T(1,128)S(1)} %reshape.3.gain_ref, bf16[32,896]{1,0:T(8,128)(2,1)S(1)} %project_out_sum.1.mine_ref.base_ref), custom_call_target="tpu_custom_call" | custom-call | flops 264241152 | bytes 8257536 | tf_op jit(solution)/shard_map/gate_up_mine/pallas_call | solution.py:618
  51.5 1.6 %gate_up_rest.1 = (bf16[8,4736]{1,0:T(8,128)(2,1)S(1)}, bf16[8,4736]{1,0:T(8,128)(2,1)S(1)}, bf16[8,4736]{1,0:T(8,128)(2,1)S(1)}, bf16[8,4736]{1,0:T(8,128)(2,1)S(1)}) custom-call(bf16[1792,2304]{1,0:T(8,128)(2,1)S(1)} %get-tuple-element.35.gate_ref, bf16[1792,2304]{1,0:T(8,128)(2,1)S(1)} %get-tuple-element.36.up_ref, f32[1,1792]{1,0:T(1,128)S(1)} %reshape.3.gain_ref, ...), custom_call_target="tpu_custom_call" | custom-call | flops 264241152 | bytes 8257536 | tf_op jit(solution)/shard_map/gate_up_rest/pallas_call | solution.py:631
  55.3 1.3 %collective-permute-start.14 = (bf16[8,4736]{1,0:T(8,128)(2,1)S(1)}, bf16[8,4736]{1,0:T(8,128)(2,1)S(1)}, u32[]{:S(2)}, u32[]{:S(2)}) collective-permute-start(bf16[8,4736]{1,0:T(8,128)(2,1)S(1)} %get-tuple-element.41), channel_id=1, source_target_pairs={{0,1},{1,0},{2,3},{3,2},{4,5},{5,4},{6,7},{7,6},{8,9},{9,8},{10,11... | collective-permute-start | bytes 227336 | tf_op jit(solution)/shard_map/ppermute | solution.py:688
  56.7 4.9 %collective-permute-done.12.rest_0_ = bf16[8,4736]{1,0:T(8,128)(2,1)S(1)} collective-permute-done((bf16[8,4736]{1,0:T(8,128)(2,1)S(1)}, bf16[8,4736]{1,0:T(8,128)(2,1)S(1)}, u32[]{:S(2)}, u32[]{:S(2)}) %collective-permute-start.12) | collective-permute-done | bytes 75808 | tf_op jit(solution)/shard_map/ppermute | solution.py:688
  61.5 1.3 %collective-permute-done.14.rest_2_ = bf16[8,4736]{1,0:T(8,128)(2,1)S(1)} collective-permute-done((bf16[8,4736]{1,0:T(8,128)(2,1)S(1)}, bf16[8,4736]{1,0:T(8,128)(2,1)S(1)}, u32[]{:S(2)}, u32[]{:S(2)}) %collective-permute-start.14) | collective-permute-done | bytes 75808 | tf_op jit(solution)/shard_map/ppermute | solution.py:688
  63.0 1.8 %collective-permute-start.15 = (bf16[8,2304]{1,0:T(8,128)(2,1)S(1)}, bf16[8,2304]{1,0:T(8,128)(2,1)S(1)}, u32[]{:S(2)}, u32[]{:S(2)}) collective-permute-start(bf16[8,2304]{1,0:T(8,128)(2,1)S(1)} %activate.1.rest_3_), channel_id=1, source_target_pairs={{0,2},{1,3},{2,0},{3,1},{4,6},{5,7},{6,4},{7,5},{8,10},{9,11},{10,... | collective-permute-start | bytes 110600 | tf_op jit(solution)/shard_map/ppermute | solution.py:688
  64.8 1.4 %collective-permute-start.16 = (bf16[8,2304]{1,0:T(8,128)(2,1)S(1)}, bf16[8,2304]{1,0:T(8,128)(2,1)S(1)}, u32[]{:S(2)}, u32[]{:S(2)}) collective-permute-start(bf16[8,2304]{1,0:T(8,128)(2,1)S(1)} %activate.1.rest_3_), channel_id=1, source_target_pairs={{0,3},{1,2},{2,1},{3,0},{4,7},{5,6},{6,5},{7,4},{8,11},{9,10},{10,... | collective-permute-start | bytes 110600 | tf_op jit(solution)/shard_map/ppermute | solution.py:688
  66.6 2.0 %collective-permute-done.15.rest_0_ = bf16[8,2304]{1,0:T(8,128)(2,1)S(1)} collective-permute-done((bf16[8,2304]{1,0:T(8,128)(2,1)S(1)}, bf16[8,2304]{1,0:T(8,128)(2,1)S(1)}, u32[]{:S(2)}, u32[]{:S(2)}) %collective-permute-start.15) | collective-permute-done | bytes 36896 | tf_op jit(solution)/shard_map/ppermute | solution.py:688
  68.5 2.1 %collective-permute-done.16.rest_1_ = bf16[8,2304]{1,0:T(8,128)(2,1)S(1)} collective-permute-done((bf16[8,2304]{1,0:T(8,128)(2,1)S(1)}, bf16[8,2304]{1,0:T(8,128)(2,1)S(1)}, u32[]{:S(2)}, u32[]{:S(2)}) %collective-permute-start.16) | collective-permute-done | bytes 36896 | tf_op jit(solution)/shard_map/ppermute | solution.py:688
  73.5 1.3 %collective-permute-start.20 = (bf16[32,896]{1,0:T(8,128)(2,1)S(1)}, bf16[32,896]{1,0:T(8,128)(2,1)S(1)}, u32[]{:S(2)}, u32[]{:S(2)}) collective-permute-start(bf16[32,896]{1,0:T(8,128)(2,1)S(1)} %add_pair.3.rest_0_), channel_id=1, source_target_pairs={{0,16},{4,20},{8,24},{12,28},{16,0},{20,4},{24,8},{28,12},{1,17},{... | collective-permute-start | bytes 172040 | tf_op jit(solution)/shard_map/ppermute | solution.py:688
  74.8 1.5 %collective-permute-start.21 = (bf16[32,896]{1,0:T(8,128)(2,1)S(1)}, bf16[32,896]{1,0:T(8,128)(2,1)S(1)}, u32[]{:S(2)}, u32[]{:S(2)}) collective-permute-start(bf16[32,896]{1,0:T(8,128)(2,1)S(1)} %add_pair.3.rest_0_), channel_id=1, source_target_pairs={{0,24},{4,28},{8,16},{12,20},{16,8},{20,12},{24,0},{28,4},{1,25},{... | collective-permute-start | bytes 172040 | tf_op jit(solution)/shard_map/ppermute | solution.py:688
  77.7 2.2 %collective-permute-done.21.rest_3_ = bf16[32,896]{1,0:T(8,128)(2,1)S(1)} collective-permute-done((bf16[32,896]{1,0:T(8,128)(2,1)S(1)}, bf16[32,896]{1,0:T(8,128)(2,1)S(1)}, u32[]{:S(2)}, u32[]{:S(2)}) %collective-permute-start.21) | collective-permute-done | bytes 57376 | tf_op jit(solution)/shard_map/ppermute | solution.py:688
  80.0 1.2 %collective-permute-done.22.sibling_ref = bf16[32,896]{1,0:T(8,128)(2,1)S(1)} collective-permute-done((bf16[32,896]{1,0:T(8,128)(2,1)S(1)}, bf16[32,896]{1,0:T(8,128)(2,1)S(1)}, u32[]{:S(2)}, u32[]{:S(2)}) %collective-permute-start.22) | collective-permute-done | bytes 57376 | tf_op jit(solution)/shard_map/ppermute | solution.py:688
  (47 shorter events, 16.3 us)
Async XLA Ops:
  17.5 2.1 %collective-permute-start = (bf16[528,512]{1,0:T(8,128)(2,1)S(1)}, bf16[528,512]{1,0:T(8,128)(2,1)S(1)}, u32[]{:S(2)}, u32[]{:S(2)}) collective-permute-start(bf16[528,512]{1,0:T(8,128)(2,1)S(1)} %get-tuple-element.28), channel_id=1, source_target_pairs={{0,4},{4,0},{8,12},{12,8},{16,20},{20,16},{24,28},{28,24},{1,5},{5... | collective-permute-start | bytes 1622024 | tf_op jit(solution)/shard_map/ppermute | solution.py:688
  20.0 7.6 %collective-permute-start.1 = (bf16[144,512]{1,0:T(8,128)(2,1)S(1)}, bf16[144,512]{1,0:T(8,128)(2,1)S(1)}, u32[]{:S(2)}, u32[]{:S(2)}) collective-permute-start(bf16[144,512]{1,0:T(8,128)(2,1)S(1)} %get-tuple-element.29), channel_id=1, source_target_pairs={{0,24},{4,28},{8,16},{12,20},{16,8},{20,12},{24,0},{28,4},{1,25},{... | collective-permute-start | bytes 442376 | tf_op jit(solution)/shard_map/ppermute | solution.py:688
  20.1 10.5 %collective-permute-start.2 = (bf16[144,512]{1,0:T(8,128)(2,1)S(1)}, bf16[144,512]{1,0:T(8,128)(2,1)S(1)}, u32[]{:S(2)}, u32[]{:S(2)}) collective-permute-start(bf16[144,512]{1,0:T(8,128)(2,1)S(1)} %get-tuple-element.30), channel_id=1, source_target_pairs={{0,16},{4,20},{8,24},{12,28},{16,0},{20,4},{24,8},{28,12},{1,17},{... | collective-permute-start | bytes 442376 | tf_op jit(solution)/shard_map/ppermute | solution.py:688
  24.3 7.2 %collective-permute-start.3 = (bf16[144,512]{1,0:T(8,128)(2,1)S(1)}, bf16[144,512]{1,0:T(8,128)(2,1)S(1)}, u32[]{:S(2)}, u32[]{:S(2)}) collective-permute-start(bf16[144,512]{1,0:T(8,128)(2,1)S(1)} %get-tuple-element.31), channel_id=1, source_target_pairs={{0,8},{4,12},{8,0},{12,4},{16,24},{20,28},{24,16},{28,20},{1,9},{5... | collective-permute-start | bytes 442376 | tf_op jit(solution)/shard_map/ppermute | solution.py:688
  32.2 5.1 %collective-permute-start.4 = (bf16[8,2048]{1,0:T(8,128)(2,1)S(1)}, bf16[8,2048]{1,0:T(8,128)(2,1)S(1)}, u32[]{:S(2)}, u32[]{:S(2)}) collective-permute-start(bf16[8,2048]{1,0:T(8,128)(2,1)S(1)} %merge_values.1.rest_3_), channel_id=1, source_target_pairs={{0,2},{1,3},{2,0},{3,1},{4,6},{5,7},{6,4},{7,5},{8,10},{9,11},{10,... | collective-permute-start | bytes 98312 | tf_op jit(solution)/shard_map/ppermute | solution.py:688
  34.9 5.7 %collective-permute-start.5 = (bf16[8,2048]{1,0:T(8,128)(2,1)S(1)}, bf16[8,2048]{1,0:T(8,128)(2,1)S(1)}, u32[]{:S(2)}, u32[]{:S(2)}) collective-permute-start(bf16[8,2048]{1,0:T(8,128)(2,1)S(1)} %merge_values.1.rest_3_), channel_id=1, source_target_pairs={{0,3},{1,2},{2,1},{3,0},{4,7},{5,6},{6,5},{7,4},{8,11},{9,10},{10,... | collective-permute-start | bytes 98312 | tf_op jit(solution)/shard_map/ppermute | solution.py:688
  36.1 4.5 %collective-permute-start.6 = (bf16[8,2048]{1,0:T(8,128)(2,1)S(1)}, bf16[8,2048]{1,0:T(8,128)(2,1)S(1)}, u32[]{:S(2)}, u32[]{:S(2)}) collective-permute-start(bf16[8,2048]{1,0:T(8,128)(2,1)S(1)} %merge_values.1.rest_3_), channel_id=1, source_target_pairs={{0,1},{1,0},{2,3},{3,2},{4,5},{5,4},{6,7},{7,6},{8,9},{9,8},{10,11... | collective-permute-start | bytes 98312 | tf_op jit(solution)/shard_map/ppermute | solution.py:688
  41.3 1.3 %collective-permute-start.7 = (bf16[32,896]{1,0:T(8,128)(2,1)S(1)}, bf16[32,896]{1,0:T(8,128)(2,1)S(1)}, u32[]{:S(2)}, u32[]{:S(2)}) collective-permute-start(bf16[32,896]{1,0:T(8,128)(2,1)S(1)} %get-tuple-element.34), channel_id=1, source_target_pairs={{0,4},{4,0},{8,12},{12,8},{16,20},{20,16},{24,28},{28,24},{1,5},{5... | collective-permute-start | bytes 172040 | tf_op jit(solution)/shard_map/ppermute | solution.py:688
  42.7 5.5 %collective-permute-start.10 = (bf16[32,896]{1,0:T(8,128)(2,1)S(1)}, bf16[32,896]{1,0:T(8,128)(2,1)S(1)}, u32[]{:S(2)}, u32[]{:S(2)}) collective-permute-start(bf16[32,896]{1,0:T(8,128)(2,1)S(1)} %add_pair.2.rest_0_), channel_id=1, source_target_pairs={{0,24},{4,28},{8,16},{12,20},{16,8},{20,12},{24,0},{28,4},{1,25},{... | collective-permute-start | bytes 172040 | tf_op jit(solution)/shard_map/ppermute | solution.py:688
  44.2 4.6 %collective-permute-start.8 = (bf16[32,896]{1,0:T(8,128)(2,1)S(1)}, bf16[32,896]{1,0:T(8,128)(2,1)S(1)}, u32[]{:S(2)}, u32[]{:S(2)}) collective-permute-start(bf16[32,896]{1,0:T(8,128)(2,1)S(1)} %add_pair.2.rest_0_), channel_id=1, source_target_pairs={{0,8},{4,12},{8,0},{12,4},{16,24},{20,28},{24,16},{28,20},{1,9},{5... | collective-permute-start | bytes 172040 | tf_op jit(solution)/shard_map/ppermute | solution.py:688
  45.6 4.2 %collective-permute-start.9 = (bf16[32,896]{1,0:T(8,128)(2,1)S(1)}, bf16[32,896]{1,0:T(8,128)(2,1)S(1)}, u32[]{:S(2)}, u32[]{:S(2)}) collective-permute-start(bf16[32,896]{1,0:T(8,128)(2,1)S(1)} %add_pair.2.rest_0_), channel_id=1, source_target_pairs={{0,16},{4,20},{8,24},{12,28},{16,0},{20,4},{24,8},{28,12},{1,17},{... | collective-permute-start | bytes 172040 | tf_op jit(solution)/shard_map/ppermute | solution.py:688
  49.8 1.7 %collective-permute-start.11 = (bf16[32,896]{1,0:T(8,128)(2,1)S(1)}, bf16[32,896]{1,0:T(8,128)(2,1)S(1)}, u32[]{:S(2)}, u32[]{:S(2)}) collective-permute-start(bf16[32,896]{1,0:T(8,128)(2,1)S(1)} %project_out_sum.1.mine_ref.base_ref), channel_id=1, source_target_pairs={{0,4},{4,0},{8,12},{12,8},{16,20},{20,16},{24,28},{28,24},{1,5},{5... | collective-permute-start | bytes 172040 | tf_op jit(solution)/shard_map/ppermute | solution.py:688
  50.0 20.6 %slice-start = ((s8[8257536]{0:T(1024)(128)(4,1)}), s8[4194304]{0:T(1024)(128)(4,1)S(1)}, s32[]{:S(2)}) async-start(s8[8257536]{0:T(1024)(128)(4,1)} %bitcast.2), calls=%async_computation | async-start | bytes 8388608
  53.1 8.4 %collective-permute-start.12 = (bf16[8,4736]{1,0:T(8,128)(2,1)S(1)}, bf16[8,4736]{1,0:T(8,128)(2,1)S(1)}, u32[]{:S(2)}, u32[]{:S(2)}) collective-permute-start(bf16[8,4736]{1,0:T(8,128)(2,1)S(1)} %get-tuple-element.39), channel_id=1, source_target_pairs={{0,2},{1,3},{2,0},{3,1},{4,6},{5,7},{6,4},{7,5},{8,10},{9,11},{10,... | collective-permute-start | bytes 227336 | tf_op jit(solution)/shard_map/ppermute | solution.py:688
  54.1 7.4 %collective-permute-start.13 = (bf16[8,4736]{1,0:T(8,128)(2,1)S(1)}, bf16[8,4736]{1,0:T(8,128)(2,1)S(1)}, u32[]{:S(2)}, u32[]{:S(2)}) collective-permute-start(bf16[8,4736]{1,0:T(8,128)(2,1)S(1)} %get-tuple-element.40), channel_id=1, source_target_pairs={{0,3},{1,2},{2,1},{3,0},{4,7},{5,6},{6,5},{7,4},{8,11},{9,10},{10,... | collective-permute-start | bytes 227336 | tf_op jit(solution)/shard_map/ppermute | solution.py:688
  55.3 7.6 %collective-permute-start.14 = (bf16[8,4736]{1,0:T(8,128)(2,1)S(1)}, bf16[8,4736]{1,0:T(8,128)(2,1)S(1)}, u32[]{:S(2)}, u32[]{:S(2)}) collective-permute-start(bf16[8,4736]{1,0:T(8,128)(2,1)S(1)} %get-tuple-element.41), channel_id=1, source_target_pairs={{0,1},{1,0},{2,3},{3,2},{4,5},{5,4},{6,7},{7,6},{8,9},{9,8},{10,11... | collective-permute-start | bytes 227336 | tf_op jit(solution)/shard_map/ppermute | solution.py:688
  63.0 5.5 %collective-permute-start.15 = (bf16[8,2304]{1,0:T(8,128)(2,1)S(1)}, bf16[8,2304]{1,0:T(8,128)(2,1)S(1)}, u32[]{:S(2)}, u32[]{:S(2)}) collective-permute-start(bf16[8,2304]{1,0:T(8,128)(2,1)S(1)} %activate.1.rest_3_), channel_id=1, source_target_pairs={{0,2},{1,3},{2,0},{3,1},{4,6},{5,7},{6,4},{7,5},{8,10},{9,11},{10,... | collective-permute-start | bytes 110600 | tf_op jit(solution)/shard_map/ppermute | solution.py:688
  64.8 5.8 %collective-permute-start.16 = (bf16[8,2304]{1,0:T(8,128)(2,1)S(1)}, bf16[8,2304]{1,0:T(8,128)(2,1)S(1)}, u32[]{:S(2)}, u32[]{:S(2)}) collective-permute-start(bf16[8,2304]{1,0:T(8,128)(2,1)S(1)} %activate.1.rest_3_), channel_id=1, source_target_pairs={{0,3},{1,2},{2,1},{3,0},{4,7},{5,6},{6,5},{7,4},{8,11},{9,10},{10,... | collective-permute-start | bytes 110600 | tf_op jit(solution)/shard_map/ppermute | solution.py:688
  66.2 4.4 %collective-permute-start.17 = (bf16[8,2304]{1,0:T(8,128)(2,1)S(1)}, bf16[8,2304]{1,0:T(8,128)(2,1)S(1)}, u32[]{:S(2)}, u32[]{:S(2)}) collective-permute-start(bf16[8,2304]{1,0:T(8,128)(2,1)S(1)} %activate.1.rest_3_), channel_id=1, source_target_pairs={{0,1},{1,0},{2,3},{3,2},{4,5},{5,4},{6,7},{7,6},{8,9},{9,8},{10,11... | collective-permute-start | bytes 110600 | tf_op jit(solution)/shard_map/ppermute | solution.py:688
  71.4 1.3 %collective-permute-start.18 = (bf16[32,896]{1,0:T(8,128)(2,1)S(1)}, bf16[32,896]{1,0:T(8,128)(2,1)S(1)}, u32[]{:S(2)}, u32[]{:S(2)}) collective-permute-start(bf16[32,896]{1,0:T(8,128)(2,1)S(1)} %get-tuple-element.44), channel_id=1, source_target_pairs={{0,4},{4,0},{8,12},{12,8},{16,20},{20,16},{24,28},{28,24},{1,5},{5... | collective-permute-start | bytes 172040 | tf_op jit(solution)/shard_map/ppermute | solution.py:688
  72.7 4.2 %collective-permute-start.19 = (bf16[32,896]{1,0:T(8,128)(2,1)S(1)}, bf16[32,896]{1,0:T(8,128)(2,1)S(1)}, u32[]{:S(2)}, u32[]{:S(2)}) collective-permute-start(bf16[32,896]{1,0:T(8,128)(2,1)S(1)} %add_pair.3.rest_0_), channel_id=1, source_target_pairs={{0,8},{4,12},{8,0},{12,4},{16,24},{20,28},{24,16},{28,20},{1,9},{5... | collective-permute-start | bytes 172040 | tf_op jit(solution)/shard_map/ppermute | solution.py:688
  73.5 4.2 %collective-permute-start.20 = (bf16[32,896]{1,0:T(8,128)(2,1)S(1)}, bf16[32,896]{1,0:T(8,128)(2,1)S(1)}, u32[]{:S(2)}, u32[]{:S(2)}) collective-permute-start(bf16[32,896]{1,0:T(8,128)(2,1)S(1)} %add_pair.3.rest_0_), channel_id=1, source_target_pairs={{0,16},{4,20},{8,24},{12,28},{16,0},{20,4},{24,8},{28,12},{1,17},{... | collective-permute-start | bytes 172040 | tf_op jit(solution)/shard_map/ppermute | solution.py:688
  74.8 5.1 %collective-permute-start.21 = (bf16[32,896]{1,0:T(8,128)(2,1)S(1)}, bf16[32,896]{1,0:T(8,128)(2,1)S(1)}, u32[]{:S(2)}, u32[]{:S(2)}) collective-permute-start(bf16[32,896]{1,0:T(8,128)(2,1)S(1)} %add_pair.3.rest_0_), channel_id=1, source_target_pairs={{0,24},{4,28},{8,16},{12,20},{16,8},{20,12},{24,0},{28,4},{1,25},{... | collective-permute-start | bytes 172040 | tf_op jit(solution)/shard_map/ppermute | solution.py:688
  79.9 1.3 %collective-permute-start.22 = (bf16[32,896]{1,0:T(8,128)(2,1)S(1)}, bf16[32,896]{1,0:T(8,128)(2,1)S(1)}, u32[]{:S(2)}, u32[]{:S(2)}) collective-permute-start(bf16[32,896]{1,0:T(8,128)(2,1)S(1)} %project_down_sum.1.mine_ref), channel_id=1, source_target_pairs={{0,4},{4,0},{8,12},{12,8},{16,20},{20,16},{24,28},{28,24},{1,5},{5... | collective-permute-start | bytes 172040 | tf_op jit(solution)/shard_map/ppermute | solution.py:688
  (3 other events, 54.3 us)
